TPU v7x, 32 devices: a whole 2x2x4 slice. The times are simulated.
32 devices in a mesh: group: 2 (over y), head: 4 (over z), req: 2 (over x), pd: 2 (over core).
Axes of the slice: x: 2, y: 2, z: 4, core: 2. Of those that a mesh axis runs over, the one named last changes fastest.
Arguments:
- x_pre: bfloat16 [32, 512, 128, 128], P(('group', 'req', 'pd'), None, 'head'), parts along dimension 0, may hold values from -6 to 6
- dt_pre: float32 [32, 512, 128], P(('group', 'req', 'pd'), None, 'head'), parts along dimension 0, may hold values from 0.002 to 0.5
- b_pre: bfloat16 [32, 512, 8, 128], P(('group', 'req', 'pd')), parts along dimension 0, may hold values from -0.5 to 0.5
- c_pre: bfloat16 [32, 512, 8, 128], P(('group', 'req', 'pd')), parts along dimension 0, may hold values from -6 to 6
- rate: float32 [128], replicated, may hold values from 0.01 to 4
- skip: float32 [128], replicated, may hold values from 0.2 to 1.5
- lengths: int32 [32], P('group'), parts along dimension 0, may hold values from 1 to 512, 4096 in all
- table: int32 [32, 16], P('group'), parts along dimension 0, may hold values from 0 to 15, each once within a row
- kv_pages: bfloat16 [32, 8, 16, 2, 32, 128], P(('group', 'req', 'pd'), None, 'head'), parts along dimension 0, may hold values from -6 to 6
- query: bfloat16 [32, 4, 8, 1024], P(('group', 'head'), None, ('req', 'pd')), parts along dimension 0, may hold values from -6 to 6
- kv_new: bfloat16 [32, 4, 8, 2, 128], P(('group', 'head'), None, ('req', 'pd')), parts along dimension 0, may hold values from -6 to 6
- x_dec: bfloat16 [32, 4, 4, 32, 128], P(('group', 'head'), None, None, ('req', 'pd')), parts along dimension 0, may hold values from -6 to 6
- dt_dec: float32 [32, 4, 4, 32], P(('group', 'head'), None, None, ('req', 'pd')), parts along dimension 0, may hold values from 0.002 to 0.5
- b_dec: bfloat16 [32, 4, 8, 128], P(('group', 'head')), parts along dimension 0, may hold values from -0.5 to 0.5
- c_dec: bfloat16 [32, 4, 8, 128], P(('group', 'head')), parts along dimension 0, may hold values from -6 to 6
Outputs:
- prefill_out: bfloat16 [32, 512, 128, 128], P(('group', 'req', 'pd'), None, 'head'), parts along dimension 0
- decode_out: bfloat16 [32, 4, 4, 32, 128], P(('group', 'head'), None, None, ('req', 'pd')), parts along dimension 0
- decode_state: float32 [32, 4, 32, 128, 128], P(('group', 'head'), None, ('req', 'pd')), parts along dimension 0
- attn_out: bfloat16 [32, 4, 8, 1024], P(('group', 'head'), None, ('req', 'pd')), parts along dimension 0
There are 2 independent parts, one for each index of `group`. A program takes and returns all parts, laid end to end along the dimension named above; an argument that names none is the same for every part. Nothing has to cross between parts.
Inputs may be any that keep to these rules, and one draw needn't show every extreme that they name: `lengths`: the longest span has exactly 512 valid tokens. `table`: each row is a permutation.
All inputs are finite; a program needn't handle non-finite values.
Results may differ from a plain program's by a relative error of at most 0.001.
Values may be sent and summed in bfloat16 or wider, within the bound.
No kernel may reach another device: no remote copies, remote signals or barrier semaphores. Data moves between devices by JAX's collectives and lax.ppermute only.
A program may use at most 256 MiB of HBM per device.

v0:
```python
import jax
import jax.numpy as jnp
from jax import lax
from jax.sharding import PartitionSpec as P

H = 128
G = 8
HEAD_SIZE = 128
BLOCK = 128
PAGE_TOKENS = 32


HIGH = lax.Precision.HIGHEST
NEG = -1e30


def span_scan(x, bh, ch, dt, rate, skip, length):
    request_count, tlen, heads, hsize = x.shape
    nstate = bh.shape[-1]
    nblk = tlen // BLOCK
    valid = jnp.arange(tlen, dtype=jnp.int32)[None, :] < length[:, None]
    dtm = jnp.where(valid[:, :, None], dt, jnp.float32(0.0))

    def blocks(arr):
        return jnp.swapaxes(arr.reshape((request_count, nblk, BLOCK) + arr.shape[2:]), 0, 1)

    tri = jnp.arange(BLOCK)[:, None] >= jnp.arange(BLOCK)[None, :]

    def step(state, blk):
        xs, bs, cs, ds = blk
        xf = xs.astype(jnp.float32)
        bf = bs.astype(jnp.float32)
        cf = cs.astype(jnp.float32)
        cum = jnp.cumsum(-rate[None, None, :] * ds, axis=1)
        diff = cum[:, :, None, :] - cum[:, None, :, :]
        mask = tri[None, :, :, None]
        seg = jnp.where(mask, jnp.exp(jnp.where(mask, diff, jnp.float32(0.0))), jnp.float32(0.0))
        scores = jnp.einsum("rthn,ruhn->rtuh", cf, bf, precision=HIGH)
        weights = seg * scores * ds[:, None, :, :]
        out = jnp.einsum("rtuh,ruhp->rthp", weights, xf, precision=HIGH)
        out = out + jnp.exp(cum)[..., None] * jnp.einsum(
            "rthn,rhpn->rthp", cf, state, precision=HIGH
        )
        out = out + skip[None, None, :, None] * xf
        tail = jnp.exp(cum[:, -1:, :] - cum) * ds
        state = jnp.exp(cum[:, -1, :])[:, :, None, None] * state + jnp.einsum(
            "ruh,ruhp,ruhn->rhpn", tail, xf, bf, precision=HIGH
        )
        return (state, out)

    start = jnp.zeros((request_count, heads, hsize, nstate), jnp.float32)
    final, outs = lax.scan(step, start, (blocks(x), blocks(bh), blocks(ch), blocks(dtm)))
    outs = jnp.swapaxes(outs, 0, 1).reshape(request_count, tlen, heads, hsize)
    outs = jnp.where(valid[:, :, None, None], outs, jnp.float32(0.0))
    return (outs.astype(jnp.bfloat16), final)


def decode_steps(state, x, bh, ch, dt, rate, skip):
    outs = []
    for step in range(x.shape[1]):
        xf = x[:, step].astype(jnp.float32)
        decay = jnp.exp(-rate[None, :] * dt[:, step])
        state = (
            decay[:, :, None, None] * state
            + dt[:, step][:, :, None, None]
            * xf[:, :, :, None]
            * bh[:, step].astype(jnp.float32)[:, :, None, :]
        )
        out = (
            jnp.einsum("rhn,rhpn->rhp", ch[:, step].astype(jnp.float32), state, precision=HIGH)
            + skip[None, :, None] * xf
        )
        outs.append(out.astype(jnp.bfloat16))
    return (jnp.stack(outs, axis=1), state)


def select_groups(proj, global_heads):
    picks = (global_heads[:, None] // (H // G) == jnp.arange(G)[None, :]).astype(jnp.bfloat16)
    return jnp.einsum("rtgn,hg->rthn", proj, picks, preferred_element_type=jnp.float32).astype(
        jnp.bfloat16
    )


def head_values(table_vec, global_heads):
    picks = (global_heads[:, None] == jnp.arange(H)[None, :]).astype(jnp.float32)
    return jnp.dot(picks, table_vec, precision=HIGH)


def page_partial(queries, page_table, positions, limit):
    request_count, key_value_heads, page_count = (
        page_table.shape[0],
        page_table.shape[1],
        page_table.shape[2],
    )
    key_rows = (
        page_table[:, :, :, 0]
        .reshape(request_count, key_value_heads, page_count * PAGE_TOKENS, HEAD_SIZE)
        .astype(jnp.float32)
    )
    value_rows = (
        page_table[:, :, :, 1]
        .reshape(request_count, key_value_heads, page_count * PAGE_TOKENS, HEAD_SIZE)
        .astype(jnp.float32)
    )
    valid = positions.reshape(request_count, page_count * PAGE_TOKENS) < limit[:, None]
    scores = jnp.einsum("rskgd,rkjd->rskgj", queries, key_rows, precision=HIGH) * (
        1.0 / HEAD_SIZE**0.5
    )
    scores = jnp.where(valid[:, None, None, None, :], scores, jnp.float32(NEG))
    top = jnp.max(scores, axis=-1)
    weights = jnp.where(
        valid[:, None, None, None, :], jnp.exp(scores - top[..., None]), jnp.float32(0.0)
    )
    return (
        top,
        jnp.sum(weights, axis=-1),
        jnp.einsum("rskgj,rkjd->rskgd", weights, value_rows, precision=HIGH),
    )


def new_partial(queries, kv_new):
    steps = kv_new.shape[1]
    key_rows = kv_new[:, :, :, 0].astype(jnp.float32)
    value_rows = kv_new[:, :, :, 1].astype(jnp.float32)
    scores = jnp.einsum("rskgd,rukd->rskgu", queries, key_rows, precision=HIGH) * (
        1.0 / HEAD_SIZE**0.5
    )
    causal = (jnp.arange(steps)[:, None] >= jnp.arange(steps)[None, :])[None, :, None, None, :]
    scores = jnp.where(causal, scores, jnp.float32(NEG))
    top = jnp.max(scores, axis=-1)
    weights = jnp.where(causal, jnp.exp(scores - top[..., None]), jnp.float32(0.0))
    return (
        top,
        jnp.sum(weights, axis=-1),
        jnp.einsum("rskgu,rukd->rskgd", weights, value_rows, precision=HIGH),
    )


def combine(first, second):
    top = jnp.maximum(first[0], second[0])
    scale_a = jnp.exp(first[0] - top)
    scale_b = jnp.exp(second[0] - top)
    return (
        top,
        first[1] * scale_a + second[1] * scale_b,
        first[2] * scale_a[..., None] + second[2] * scale_b[..., None],
    )


def page_positions(rows):
    return rows[:, :, None] * PAGE_TOKENS + jnp.arange(PAGE_TOKENS, dtype=jnp.int32)[None, None, :]


def moved_pages(page_table, queries, table, dec_start, dec_lengths, n_head):
    dec_reqs, kv_local, page_local = (queries.shape[0], queries.shape[2], page_table.shape[2])
    page_table = page_table.reshape((dec_reqs, n_head, kv_local) + page_table.shape[2:])
    page_table = jnp.swapaxes(page_table, 1, 2)
    page_table = page_table.reshape(
        (dec_reqs, kv_local, n_head * page_local) + page_table.shape[4:]
    )
    dec_rows = lax.dynamic_slice_in_dim(table, dec_start, dec_reqs, 0)
    return page_partial(queries, page_table, page_positions(dec_rows), dec_lengths)


def local(
    x_pre,
    dt_pre,
    b_pre,
    c_pre,
    rate,
    skip,
    lengths,
    table,
    kv_pages,
    query,
    kv_new,
    x_dec,
    dt_dec,
    b_dec,
    c_dec,
):
    n_head = lax.axis_size("head")
    n_split = lax.axis_size(("req", "pd"))
    head_idx = lax.axis_index("head")
    split_idx = lax.axis_index(("req", "pd"))
    r_dev = x_pre.shape[0]
    local_heads = x_pre.shape[2]
    part_heads = local_heads // n_split
    dec_reqs = query.shape[0]
    kv_local = query.shape[2]
    group_q = query.shape[3] // HEAD_SIZE
    steps = query.shape[1]
    pre_heads = head_idx * local_heads + jnp.arange(local_heads, dtype=jnp.int32)
    my_lengths = lax.dynamic_slice_in_dim(lengths, split_idx * r_dev, r_dev, 0)
    prefill_out, final = span_scan(
        x_pre,
        select_groups(b_pre, pre_heads),
        select_groups(c_pre, pre_heads),
        dt_pre,
        head_values(rate, pre_heads),
        head_values(skip, pre_heads),
        my_lengths,
    )
    dec_start = head_idx * dec_reqs
    dec_lengths = lax.dynamic_slice_in_dim(lengths, dec_start, dec_reqs, 0)
    queries = query.reshape(dec_reqs, steps, kv_local, group_q, HEAD_SIZE).astype(jnp.float32)
    states, page_table = (
        lax.all_to_all(final, ("req", "pd"), split_axis=1, concat_axis=0, tiled=True),
        lax.all_to_all(
            kv_pages.astype(jnp.float32), ("req", "pd"), split_axis=1, concat_axis=0, tiled=True
        ).astype(kv_pages.dtype),
    )
    states, page_table = (
        lax.all_to_all(states, "head", split_axis=0, concat_axis=1, tiled=True),
        lax.all_to_all(
            page_table.astype(jnp.float32), "head", split_axis=0, concat_axis=1, tiled=True
        ).astype(page_table.dtype),
    )
    cached = moved_pages(page_table, queries, table, dec_start, dec_lengths, n_head)
    total = combine(cached, new_partial(queries, kv_new))
    attn_out = (
        (total[2] / total[1][..., None])
        .reshape(dec_reqs, steps, kv_local, group_q * HEAD_SIZE)
        .astype(jnp.bfloat16)
    )
    dec_heads = (
        jnp.arange(n_head, dtype=jnp.int32)[:, None] * local_heads
        + split_idx * part_heads
        + jnp.arange(part_heads, dtype=jnp.int32)[None, :]
    ).reshape(-1)
    xd = x_dec.reshape(dec_reqs, steps, n_head * part_heads, x_dec.shape[-1])
    dtd = dt_dec.reshape(dec_reqs, steps, n_head * part_heads)
    dec_out, dec_state = decode_steps(
        states,
        xd,
        select_groups(b_dec, dec_heads),
        select_groups(c_dec, dec_heads),
        dtd,
        head_values(rate, dec_heads),
        head_values(skip, dec_heads),
    )
    decode_out = dec_out.reshape(x_dec.shape)
    decode_state = dec_state.reshape(
        dec_reqs, n_head, part_heads, dec_state.shape[-2], dec_state.shape[-1]
    )
    return (prefill_out, decode_out, decode_state, attn_out)


def solution(mesh):
    placed = (
        P(("group", "req", "pd"), None, "head", None),
        P(("group", "req", "pd"), None, "head"),
        P(("group", "req", "pd"), None, None, None),
        P(("group", "req", "pd"), None, None, None),
        P(),
        P(),
        P("group"),
        P("group", None),
        P(("group", "req", "pd"), None, "head", None, None, None),
        P(("group", "head"), None, ("req", "pd"), None),
        P(("group", "head"), None, ("req", "pd"), None, None),
        P(("group", "head"), None, None, ("req", "pd"), None),
        P(("group", "head"), None, None, ("req", "pd")),
        P(("group", "head"), None, None, None),
        P(("group", "head"), None, None, None),
    )
    return jax.shard_map(
        local,
        mesh=mesh,
        in_specs=placed,
        out_specs=(
            P(("group", "req", "pd"), None, "head", None),
            P(("group", "head"), None, None, ("req", "pd"), None),
            P(("group", "head"), None, ("req", "pd"), None, None),
            P(("group", "head"), None, ("req", "pd"), None),
        ),
        check_vma=False,
    )
```

profile of v0, /device:TPU:0, one launch (start us, length us, event | category | flops | bytes accessed | tf_op | source)
XLA Modules:
  0.0 772.2 jit_solution(7777254277461962409)
XLA Ops:
  11.3 9.7 %convolution_convert_fusion.1 = bf16[32,4,512,128]{3,0,2,1:T(8,128)(2,1)} fusion(bf16[4,512,8,128]{3,2,1,0:T(8,128)(2,1)} %param.19, s32[32]{0:T(128)S(1)} %get-tuple-element.294), kind=kOutput, calls=%fused_computation.52 | convolution fusion | flops 142606592 | bytes 20971648 | tf_op jit(solution)/shard_map/rtgn,hg->rthn/dot_general | solution.py:79
  21.0 17.7 %copy.240 = bf16[4,4,128,32,128]{4,2,3,0,1:T(8,128)(2,1)} copy(bf16[4,4,128,32,128]{4,3,2,1,0:T(8,128)(2,1)} %bitcast.371) | data formatting | bytes 33554432 | tf_op jit(solution)/shard_map/reshape | solution.py:25
  38.7 8.1 %convolution_convert_fusion = bf16[32,4,512,128]{3,0,2,1:T(8,128)(2,1)} fusion(bf16[4,512,8,128]{3,2,1,0:T(8,128)(2,1)S(1)} %copy-done.1, s32[32]{0:T(128)S(1)} %get-tuple-element.294), kind=kOutput, calls=%fused_computation.51 | convolution fusion | flops 142606592 | bytes 20971648 | tf_op jit(solution)/shard_map/rtgn,hg->rthn/dot_general | solution.py:79
  46.8 17.6 %copy.239 = bf16[4,4,128,32,128]{4,2,3,0,1:T(8,128)(2,1)} copy(bf16[4,4,128,32,128]{4,3,2,1,0:T(8,128)(2,1)} %bitcast.370) | data formatting | bytes 33554432 | tf_op jit(solution)/shard_map/reshape | solution.py:25
  64.7 281.1 %while.16 = (s32[]{:T(128)}, f32[4,32,128,128]{3,2,1,0:T(8,128)}, bf16[4,4,128,32,128]{2,4,3,1,0:T(8,128)(2,1)}, f32[1,1,32]{2,1,0:T(1,128)S(1)}, f32[4,4,128,32...) while((s32[]{:T(128)}, f32[4,32,128,128]{3,2,1,0:T(8,128)}, ...), condition=%wide.region_2.3_spmd.clone.clone, body=%wide.region_0.2_spmd.clone.clone.sunk | while | flops 10236248064 | bytes 114791192 | solution.py:52
  65.0 14.3 %fusion.179 = f32[4,32,128,128]{2,3,1,0:T(8,128)} fusion(f32[4,32,128,128]{3,2,1,0:T(8,128)} %get-tuple-element.377, pred[]{:T(512)S(6)} %compare.21, bf16[4,4,128,32,128]{4,2,3,1,0:T(8,128)(2,1)} %get-tuple-element.395, s32[]{:T(128)S(6)} %copy.256), kind=kOutput, calls=%fused_computation.17.clone.1 | convolution fusion | flops 3223322624 | bytes 20971524 | tf_op jit(solution)/shard_map/while/body/eval_jaxpr/rthn,rhpn->rthp/dot_general | solution.py:41
  84.8 7.9 %copy.248 = bf16[1,4,128,32,128]{2,4,3,1,0:T(8,128)(2,1)} copy(bf16[1,4,128,32,128]{4,3,2,0,1:T(8,128)(2,1)} %constant_dynamic-slice_fusion.5) | data formatting | bytes 8388608 | tf_op jit(solution)/shard_map/while/body/jit(dynamic_index_in_dim)/dynamic_slice | solution.py:52
  92.9 11.9 %multiply_add_fusion.14 = f32[4,32,128,128]{3,2,1,0:T(8,128)} fusion(f32[4,32,128,128]{3,2,1,0:T(8,128)} %get-tuple-element.377, f32[4,32]{1,0:T(4,128)S(1)} %exp.147, pred[]{:T(512)S(6)} %compare.21, bf16[4,4,128,32,128]{4,2,3,1,0:T(8,128)(2,1)} %get-tuple-element.394, s32[]{:T(128)S(6)} %copy.256, bf16[1,4,128,32,128]{2,4,3,1,0:T(8,128)(2,1)} %copy.248, ...), kind=kOutput, calls=%fused_computation.16.clone.1 | convolution fusion | flops 3231711232 | bytes 25231876 | tf_op jit(solution)/shard_map/while/body/eval_jaxpr/ruh,ruhp,ruhn->rhpn/dot_general | solution.py:46
  104.8 9.7 %fusion.180 = f32[4,32,128,128]{3,2,1,0:T(8,128)} fusion(bf16[4,4,128,32,128]{4,2,3,1,0:T(8,128)(2,1)} %get-tuple-element.395, s32[]{:T(128)S(6)} %copy.256, bf16[4,4,128,32,128]{4,2,3,1,0:T(8,128)(2,1)} %get-tuple-element.394), kind=kOutput, calls=%fused_computation.20.clone.1 | convolution fusion | flops 536870912 | bytes 16778240 | tf_op jit(solution)/shard_map/while/body/eval_jaxpr/rthn,ruhn->rtuh/dot_general | solution.py:38
  114.7 14.3 %fusion.181 = bf16[4,4,128,32,128]{2,4,3,1,0:T(8,128)(2,1)} fusion(bf16[4,4,128,32,128]{2,4,3,1,0:T(8,128)(2,1)} %get-tuple-element.378, s32[]{:T(128)S(6)} %copy.256, f32[4,32,128,128]{2,3,1,0:T(8,128)} %fusion.179, f32[4,32,128,128]{3,2,1,0:T(8,128)} %fusion.180, bf16[1,4,128,32,128]{2,4,3,1,0:T(8,128)(2,1)} %copy.248, ...), kind=kOutput, calls=%fused_computation.6.clone.1 | convolution fusion | flops 3242196992 | bytes 33833476 | tf_op jit(solution)/shard_map/while/body/eval_jaxpr/rtuh,ruhp->rthp/dot_general | solution.py:40
  129.0 16.7 %fusion.179 = f32[4,32,128,128]{2,3,1,0:T(8,128)} fusion(f32[4,32,128,128]{3,2,1,0:T(8,128)} %get-tuple-element.377, pred[]{:T(512)S(6)} %compare.21, bf16[4,4,128,32,128]{4,2,3,1,0:T(8,128)(2,1)} %get-tuple-element.395, s32[]{:T(128)S(6)} %copy.256), kind=kOutput, calls=%fused_computation.17.clone.1 | convolution fusion | flops 3223322624 | bytes 20971524 | tf_op jit(solution)/shard_map/while/body/eval_jaxpr/rthn,rhpn->rthp/dot_general | solution.py:41
  159.4 14.3 %multiply_add_fusion.14 = f32[4,32,128,128]{3,2,1,0:T(8,128)} fusion(f32[4,32,128,128]{3,2,1,0:T(8,128)} %get-tuple-element.377, f32[4,32]{1,0:T(4,128)S(1)} %exp.147, pred[]{:T(512)S(6)} %compare.21, bf16[4,4,128,32,128]{4,2,3,1,0:T(8,128)(2,1)} %get-tuple-element.394, s32[]{:T(128)S(6)} %copy.256, bf16[1,4,128,32,128]{2,4,3,1,0:T(8,128)(2,1)} %copy.248, ...), kind=kOutput, calls=%fused_computation.16.clone.1 | convolution fusion | flops 3231711232 | bytes 25231876 | tf_op jit(solution)/shard_map/while/body/eval_jaxpr/ruh,ruhp,ruhn->rhpn/dot_general | solution.py:46
  173.6 9.7 %fusion.180 = f32[4,32,128,128]{3,2,1,0:T(8,128)} fusion(bf16[4,4,128,32,128]{4,2,3,1,0:T(8,128)(2,1)} %get-tuple-element.395, s32[]{:T(128)S(6)} %copy.256, bf16[4,4,128,32,128]{4,2,3,1,0:T(8,128)(2,1)} %get-tuple-element.394), kind=kOutput, calls=%fused_computation.20.clone.1 | convolution fusion | flops 536870912 | bytes 16778240 | tf_op jit(solution)/shard_map/while/body/eval_jaxpr/rthn,ruhn->rtuh/dot_general | solution.py:38
  183.6 14.3 %fusion.181 = bf16[4,4,128,32,128]{2,4,3,1,0:T(8,128)(2,1)} fusion(bf16[4,4,128,32,128]{2,4,3,1,0:T(8,128)(2,1)} %get-tuple-element.378, s32[]{:T(128)S(6)} %copy.256, f32[4,32,128,128]{2,3,1,0:T(8,128)} %fusion.179, f32[4,32,128,128]{3,2,1,0:T(8,128)} %fusion.180, bf16[1,4,128,32,128]{2,4,3,1,0:T(8,128)(2,1)} %copy.248, ...), kind=kOutput, calls=%fused_computation.6.clone.1 | convolution fusion | flops 3242196992 | bytes 33833476 | tf_op jit(solution)/shard_map/while/body/eval_jaxpr/rtuh,ruhp->rthp/dot_general | solution.py:40
  197.9 16.7 %fusion.179 = f32[4,32,128,128]{2,3,1,0:T(8,128)} fusion(f32[4,32,128,128]{3,2,1,0:T(8,128)} %get-tuple-element.377, pred[]{:T(512)S(6)} %compare.21, bf16[4,4,128,32,128]{4,2,3,1,0:T(8,128)(2,1)} %get-tuple-element.395, s32[]{:T(128)S(6)} %copy.256), kind=kOutput, calls=%fused_computation.17.clone.1 | convolution fusion | flops 3223322624 | bytes 20971524 | tf_op jit(solution)/shard_map/while/body/eval_jaxpr/rthn,rhpn->rthp/dot_general | solution.py:41
  228.2 14.3 %multiply_add_fusion.14 = f32[4,32,128,128]{3,2,1,0:T(8,128)} fusion(f32[4,32,128,128]{3,2,1,0:T(8,128)} %get-tuple-element.377, f32[4,32]{1,0:T(4,128)S(1)} %exp.147, pred[]{:T(512)S(6)} %compare.21, bf16[4,4,128,32,128]{4,2,3,1,0:T(8,128)(2,1)} %get-tuple-element.394, s32[]{:T(128)S(6)} %copy.256, bf16[1,4,128,32,128]{2,4,3,1,0:T(8,128)(2,1)} %copy.248, ...), kind=kOutput, calls=%fused_computation.16.clone.1 | convolution fusion | flops 3231711232 | bytes 25231876 | tf_op jit(solution)/shard_map/while/body/eval_jaxpr/ruh,ruhp,ruhn->rhpn/dot_general | solution.py:46
  242.5 9.7 %fusion.180 = f32[4,32,128,128]{3,2,1,0:T(8,128)} fusion(bf16[4,4,128,32,128]{4,2,3,1,0:T(8,128)(2,1)} %get-tuple-element.395, s32[]{:T(128)S(6)} %copy.256, bf16[4,4,128,32,128]{4,2,3,1,0:T(8,128)(2,1)} %get-tuple-element.394), kind=kOutput, calls=%fused_computation.20.clone.1 | convolution fusion | flops 536870912 | bytes 16778240 | tf_op jit(solution)/shard_map/while/body/eval_jaxpr/rthn,ruhn->rtuh/dot_general | solution.py:38
  252.5 14.3 %fusion.181 = bf16[4,4,128,32,128]{2,4,3,1,0:T(8,128)(2,1)} fusion(bf16[4,4,128,32,128]{2,4,3,1,0:T(8,128)(2,1)} %get-tuple-element.378, s32[]{:T(128)S(6)} %copy.256, f32[4,32,128,128]{2,3,1,0:T(8,128)} %fusion.179, f32[4,32,128,128]{3,2,1,0:T(8,128)} %fusion.180, bf16[1,4,128,32,128]{2,4,3,1,0:T(8,128)(2,1)} %copy.248, ...), kind=kOutput, calls=%fused_computation.6.clone.1 | convolution fusion | flops 3242196992 | bytes 33833476 | tf_op jit(solution)/shard_map/while/body/eval_jaxpr/rtuh,ruhp->rthp/dot_general | solution.py:40
  266.8 16.7 %fusion.179 = f32[4,32,128,128]{2,3,1,0:T(8,128)} fusion(f32[4,32,128,128]{3,2,1,0:T(8,128)} %get-tuple-element.377, pred[]{:T(512)S(6)} %compare.21, bf16[4,4,128,32,128]{4,2,3,1,0:T(8,128)(2,1)} %get-tuple-element.395, s32[]{:T(128)S(6)} %copy.256), kind=kOutput, calls=%fused_computation.17.clone.1 | convolution fusion | flops 3223322624 | bytes 20971524 | tf_op jit(solution)/shard_map/while/body/eval_jaxpr/rthn,rhpn->rthp/dot_general | solution.py:41
  297.1 14.3 %multiply_add_fusion.14 = f32[4,32,128,128]{3,2,1,0:T(8,128)} fusion(f32[4,32,128,128]{3,2,1,0:T(8,128)} %get-tuple-element.377, f32[4,32]{1,0:T(4,128)S(1)} %exp.147, pred[]{:T(512)S(6)} %compare.21, bf16[4,4,128,32,128]{4,2,3,1,0:T(8,128)(2,1)} %get-tuple-element.394, s32[]{:T(128)S(6)} %copy.256, bf16[1,4,128,32,128]{2,4,3,1,0:T(8,128)(2,1)} %copy.248, ...), kind=kOutput, calls=%fused_computation.16.clone.1 | convolution fusion | flops 3231711232 | bytes 25231876 | tf_op jit(solution)/shard_map/while/body/eval_jaxpr/ruh,ruhp,ruhn->rhpn/dot_general | solution.py:46
  311.4 9.7 %fusion.180 = f32[4,32,128,128]{3,2,1,0:T(8,128)} fusion(bf16[4,4,128,32,128]{4,2,3,1,0:T(8,128)(2,1)} %get-tuple-element.395, s32[]{:T(128)S(6)} %copy.256, bf16[4,4,128,32,128]{4,2,3,1,0:T(8,128)(2,1)} %get-tuple-element.394), kind=kOutput, calls=%fused_computation.20.clone.1 | convolution fusion | flops 536870912 | bytes 16778240 | tf_op jit(solution)/shard_map/while/body/eval_jaxpr/rthn,ruhn->rtuh/dot_general | solution.py:38
  321.4 14.3 %fusion.181 = bf16[4,4,128,32,128]{2,4,3,1,0:T(8,128)(2,1)} fusion(bf16[4,4,128,32,128]{2,4,3,1,0:T(8,128)(2,1)} %get-tuple-element.378, s32[]{:T(128)S(6)} %copy.256, f32[4,32,128,128]{2,3,1,0:T(8,128)} %fusion.179, f32[4,32,128,128]{3,2,1,0:T(8,128)} %fusion.180, bf16[1,4,128,32,128]{2,4,3,1,0:T(8,128)(2,1)} %copy.248, ...), kind=kOutput, calls=%fused_computation.6.clone.1 | convolution fusion | flops 3242196992 | bytes 33833476 | tf_op jit(solution)/shard_map/while/body/eval_jaxpr/rtuh,ruhp->rthp/dot_general | solution.py:40
  363.1 89.9 %all-to-all-done = f32[4,32,128,128]{3,2,0,1:T(8,128)} async-done(((f32[4,32,128,128]{3,2,0,1:T(8,128)}), f32[4,32,128,128]{3,2,0,1:T(8,128)}, u32[]{:S(2)}, u32[]{:S(2)}) %all-to-all-start) | async-done | bytes 8388640 | tf_op jit(solution)/shard_map/all_to_all | solution.py:208
  458.7 7.9 %copy.136 = f32[4,4,8,128,128]{4,3,2,1,0:T(8,128)} copy(f32[4,4,8,128,128]{4,3,1,2,0:T(8,128)} %bitcast.29) | data formatting | bytes 16777216 | tf_op jit(solution)/shard_map/all_to_all | solution.py:208
  466.6 40.1 %all-to-all-done.3 = bf16[16,2,4,2,32,128]{5,4,3,2,1,0:T(8,128)(2,1)S(1)} async-done(((bf16[16,2,4,2,32,128]{5,4,3,2,1,0:T(8,128)(2,1)}), bf16[16,2,4,2,32,128]{5,4,3,2,1,0:T(8,128)(2,1)S(1)}, u32[]{:S(2)}, u32[]{:S(2)}) %all-to-all-start.3) | async-done | bytes 2097184 | tf_op jit(solution)/shard_map/all_to_all | solution.py:215
  512.5 28.0 %copy.132 = bf16[4,4,128,32,128]{4,3,2,1,0:T(8,128)(2,1)} copy(bf16[4,4,128,32,128]{2,4,3,0,1:T(8,128)(2,1)} %bitcast.378) | data formatting | bytes 33554432 | tf_op jit(solution)/shard_map/transpose | solution.py:53
  545.1 15.1 %select_convert_fusion = bf16[4,512,32,128]{3,2,1,0:T(8,128)(2,1)} fusion(bf16[4,512,32,128]{3,2,1,0:T(8,128)(2,1)} %bitcast.369, pred[4,512]{1,0:T(4,128)(4,1)S(1)} %copy-done.11), kind=kLoop, calls=%fused_computation.48 | loop fusion | flops 8388608 | bytes 33556480 | tf_op jit(solution)/shard_map/convert_element_type | solution.py:55
  563.8 131.2 %all-to-all-done.1 = f32[16,8,128,128]{3,2,1,0:T(8,128)} async-done(((f32[16,8,128,128]{3,2,1,0:T(8,128)}), f32[16,8,128,128]{3,2,1,0:T(8,128)}, u32[]{:S(2)}, u32[]{:S(2)}) %all-to-all-start.1) | async-done | bytes 8388640 | tf_op jit(solution)/shard_map/all_to_all | solution.py:214
  699.0 14.0 %multiply_add_fusion.1 = f32[4,4,8,128,128]{4,3,2,0,1:T(8,128)S(1)} fusion(f32[4,4,8,128,128]{4,3,2,0,1:T(8,128)} %bitcast.32, f32[4,4,8]{2,0,1:T(4,128)S(1)} %copy.149, f32[4,4,8]{2,0,1:T(4,128)S(1)} %copy.148, f32[4,4,8]{2,0,1:T(4,128)S(1)} %copy.147, f32[4,4,8]{2,0,1:T(4,128)S(1)} %copy.146, f32[4,4,8,128]{3,2,1,0:T(8,128)S(1)} %get-tuple-element.254, ...), kind=kLoop, calls=%fused_computation.53 | loop fusion | flops 25165824 | bytes 17303552 | tf_op jit(solution)/shard_map/add | solution.py:64
  724.7 12.1 %fusion.62 = f32[4,32,1,128]{3,2,1,0:T(1,128)S(1)} fusion(f32[4,32,128,128]{3,2,1,0:T(8,128)S(1)} %bitcast.374, f32[4,32,128]{2,1,0:T(8,128)S(1)} %get-tuple-element.264, f32[4,32,128]{2,1,0:T(8,128)S(1)} %get-tuple-element.273, f32[4,32]{1,0:T(4,128)S(1)} %get-tuple-element.287, f32[4,32,128]{2,1,0:T(8,128)S(1)} %get-tuple-element.265, ...), kind=kOutput, calls=%fused_computation.77 | convolution fusion | flops 37748736 | bytes 8750080 | tf_op jit(solution)/shard_map/rhn,rhpn->rhp/dot_general | solution.py:70
  736.8 14.4 %fusion.49 = f32[4,32,1,128]{3,2,1,0:T(1,128)S(1)} fusion(f32[4,32,128]{2,1,0:T(8,128)S(1)} %get-tuple-element.263, f32[4,32,128]{2,1,0:T(8,128)S(1)} %get-tuple-element.272, f32[4,32]{1,0:T(4,128)S(1)} %get-tuple-element.288, f32[4,32,128,128]{3,2,1,0:T(8,128)S(1)} %bitcast.375, f32[4,32,128]{2,1,0:T(8,128)S(1)} %get-tuple-element.264, ...), kind=kOutput, calls=%fused_computation.62 | convolution fusion | flops 44040192 | bytes 8881664 | tf_op jit(solution)/shard_map/rhn,rhpn->rhp/dot_general | solution.py:70
  751.3 19.9 %fusion.44 = f32[4,32,1,128]{3,2,1,0:T(1,128)S(1)} fusion(f32[4,32,128]{2,1,0:T(8,128)S(1)} %get-tuple-element.262, f32[4,32,128]{2,1,0:T(8,128)S(1)} %get-tuple-element.271, f32[4,32]{1,0:T(4,128)S(1)} %copy-done.12, f32[4,32,128]{2,1,0:T(8,128)S(1)} %get-tuple-element.263, f32[4,32,128]{2,1,0:T(8,128)S(1)} %get-tuple-element.272, ...), kind=kOutput, calls=%fused_computation.54 | convolution fusion | flops 50331648 | bytes 9013248 | tf_op jit(solution)/shard_map/rhn,rhpn->rhp/dot_general | solution.py:70
  (158 shorter events, 111.4 us)
Async XLA Ops:
  0.6 543.0 %copy-start = (bf16[4,4,8,128]{3,2,1,0:T(8,128)(2,1)S(1)}, bf16[4,4,8,128]{3,2,1,0:T(8,128)(2,1)}, u32[]{:S(2)}) copy-start(bf16[4,4,8,128]{3,2,1,0:T(8,128)(2,1)} %param.31) | copy-start | bytes 98308
  0.6 9.2 %copy-start.13 = (s32[16]{0:T(128)S(1)}, s32[16]{0:T(128)}, u32[]{:S(2)}) copy-start(s32[16]{0:T(128)} %param.23) | copy-start | bytes 196
  0.7 10.5 %copy-start.2 = (f32[4,512,32]{1,2,0:T(8,128)S(1)}, f32[4,512,32]{1,2,0:T(8,128)}, u32[]{:S(2)}) copy-start(f32[4,512,32]{1,2,0:T(8,128)} %param.18) | copy-start | bytes 786436
  4.4 349.2 %all-to-all-start.2 = ((bf16[4,8,4,2,32,128]{5,4,3,2,0,1:T(8,128)(2,1)}), bf16[4,8,4,2,32,128]{5,4,3,2,0,1:T(8,128)(2,1)}, u32[]{:S(2)}, u32[]{:S(2)}) async-start(bf16[4,8,4,2,32,128]{5,4,3,2,0,1:T(8,128)(2,1)} %copy.216), calls=%async_computation.2 | async-start | bytes 4194304 | tf_op jit(solution)/shard_map/all_to_all | solution.py:209
  10.5 0.6 copy-start.10
  21.0 17.7 %copy-start.1 = (bf16[4,512,8,128]{3,2,1,0:T(8,128)(2,1)S(1)}, bf16[4,512,8,128]{3,2,1,0:T(8,128)(2,1)}, u32[]{:S(2)}) copy-start(bf16[4,512,8,128]{3,2,1,0:T(8,128)(2,1)} %param.20) | copy-start | bytes 12582916
  46.8 17.6 %copy-start.15 = (f32[128]{0:T(128)S(1)}, f32[128]{0:T(128)}, u32[]{:S(2)}) copy-start(f32[128]{0:T(128)} %param.21) | copy-start | bytes 1540
  46.8 17.8 %copy-start.17 = (f32[128]{0:T(128)S(1)}, f32[128]{0:T(128)}, u32[]{:S(2)}) copy-start(f32[128]{0:T(128)} %param.22) | copy-start | bytes 1540
  353.6 99.4 %all-to-all-start = ((f32[4,32,128,128]{3,2,0,1:T(8,128)}), f32[4,32,128,128]{3,2,0,1:T(8,128)}, u32[]{:S(2)}, u32[]{:S(2)}) async-start(f32[4,32,128,128]{3,2,0,1:T(8,128)} %copy.134), calls=%async_computation | async-start | bytes 16777216 | tf_op jit(solution)/shard_map/all_to_all | solution.py:208
  453.0 53.8 %all-to-all-start.3 = ((bf16[16,2,4,2,32,128]{5,4,3,2,1,0:T(8,128)(2,1)}), bf16[16,2,4,2,32,128]{5,4,3,2,1,0:T(8,128)(2,1)S(1)}, u32[]{:S(2)}, u32[]{:S(2)}) async-start(bf16[16,2,4,2,32,128]{5,4,3,2,1,0:T(8,128)(2,1)} %bitcast.380), calls=%async_computation.3 | async-start | bytes 4194304 | tf_op jit(solution)/shard_map/all_to_all | solution.py:215
  506.7 188.2 %all-to-all-start.1 = ((f32[16,8,128,128]{3,2,1,0:T(8,128)}), f32[16,8,128,128]{3,2,1,0:T(8,128)}, u32[]{:S(2)}, u32[]{:S(2)}) async-start(f32[16,8,128,128]{3,2,1,0:T(8,128)} %bitcast.372), calls=%async_computation.1 | async-start | bytes 16777216 | tf_op jit(solution)/shard_map/all_to_all | solution.py:214
  512.4 28.3 %copy-start.7 = (f32[4,4,4,8]{3,2,1,0:T(4,128)S(1)}, f32[4,4,4,8]{3,2,1,0:T(4,128)}, u32[]{:S(2)}) copy-start(f32[4,4,4,8]{3,2,1,0:T(4,128)} %param.29) | copy-start | bytes 6148
  512.4 28.4 %copy-start.3 = (bf16[4,4,4,8,128]{4,3,2,1,0:T(8,128)(2,1)S(1)}, bf16[4,4,4,8,128]{4,3,2,1,0:T(8,128)(2,1)}, u32[]{:S(2)}) copy-start(bf16[4,4,4,8,128]{4,3,2,1,0:T(8,128)(2,1)} %param.28) | copy-start | bytes 393220
  512.4 28.5 %copy-start.16 = (f32[128]{0:T(128)S(1)}, f32[128]{0:T(128)}, u32[]{:S(2)}) copy-start(f32[128]{0:T(128)} %param.21) | copy-start | bytes 1540
  512.4 29.1 %copy-start.4 = (bf16[4,4,2,1024]{3,2,1,0:T(2,128)(2,1)S(1)}, bf16[4,4,2,1024]{3,2,1,0:T(2,128)(2,1)}, u32[]{:S(2)}) copy-start(bf16[4,4,2,1024]{3,2,1,0:T(2,128)(2,1)} %param.26) | copy-start | bytes 196612
  512.5 29.2 %copy-start.18 = (f32[128]{0:T(128)S(1)}, f32[128]{0:T(128)}, u32[]{:S(2)}) copy-start(f32[128]{0:T(128)} %param.22) | copy-start | bytes 1540
  512.5 29.9 %copy-start.5 = (bf16[4,4,2,2,128]{4,3,2,1,0:T(2,128)(2,1)S(1)}, bf16[4,4,2,2,128]{4,3,2,1,0:T(2,128)(2,1)}, u32[]{:S(2)}) copy-start(bf16[4,4,2,2,128]{4,3,2,1,0:T(2,128)(2,1)} %param.27) | copy-start | bytes 49156
  512.5 32.0 %copy-start.6 = (bf16[4,4,8,128]{3,2,1,0:T(8,128)(2,1)S(1)}, bf16[4,4,8,128]{3,2,1,0:T(8,128)(2,1)}, u32[]{:S(2)}) copy-start(bf16[4,4,8,128]{3,2,1,0:T(8,128)(2,1)} %param.30) | copy-start | bytes 98308
  512.5 32.6 %copy-start.11 = (pred[4,512]{1,0:T(4,128)(4,1)S(1)}, pred[4,512]{1,0:T(4,128)(4,1)}, u32[]{:S(2)}) copy-start(pred[4,512]{1,0:T(4,128)(4,1)} %copy-done.10) | copy-start | bytes 6148
  560.1 1.0 copy-start.9
  717.0 7.7 copy-start.8
  736.8 14.4 %copy-start.12 = (f32[4,32]{1,0:T(4,128)S(1)}, f32[4,32]{1,0:T(4,128)}, u32[]{:S(2)}) copy-start(f32[4,32]{1,0:T(4,128)} %get-tuple-element.289) | copy-start | bytes 1540
  751.2 19.9 %copy-start.14 = (f32[32]{0:T(128)S(1)}, f32[32]{0:T(128)}, u32[]{:S(2)}) copy-start(f32[32]{0:T(128)} %convolution_bitcast_fusion.2) | copy-start | bytes 388
where the time goes:
time: 775 us; the launch traced here: 772 us
  matrix products  291 us (38%)
  waiting for transfers between devices  261 us (34%)
  local copies, waits for them, and re-layouts  152 us (20%)
  other arithmetic  34.3 us (4%)
  starting transfers between devices  21.5 us (3%)
  loops' own time  10.5 us (1%)
    all_to_all x1, waiting for transfers between devices, local(): lax.all_to_all(states, 'head', split_axis=0, concat_axis=1, tiled=True)  131 us
    all_to_all x1, waiting for transfers between devices, local(): lax.all_to_all(final, ('req', 'pd'), split_axis=1, concat_axis=0, tiled=T...  89.9 us
    dot_general x4, matrix products, step(): jnp.einsum('rthn,rhpn->rthp', cf, state, precision=HIGH)  64.4 us
    dot_general x4, matrix products, step(): out = jnp.einsum('rtuh,ruhp->rthp', weights, xf, precision=HIGH)  57.4 us
    dot_general x4, matrix products, step(): jnp.einsum('ruh,ruhp,ruhn->rhpn', tail, xf, bf, precision=HIGH)  54.7 us
    dot_general x4, matrix products, decode_steps(): jnp.einsum('rhn,rhpn->rhp', ch[:, step].astype(jnp.float32), state, preci...  54.1 us
    dynamic_slice x16, local copies, waits for them, and re-layouts, span_scan(): lax.scan(step, start, (blocks(x), blocks(bh), blocks(ch), blocks(dtm)))  52.4 us
    all_to_all x1, waiting for transfers between devices, local(): lax.all_to_all(page_table.astype(jnp.float32), 'head', split_axis=0, conc...  40.1 us
  transfers between devices with their start and end apart: 4, of which 3 were waited for; matrix products, arithmetic and copies ran while one was open for 51% of the time, Pallas kernels for 0%

commit v1 on v0

v1 whole, which is shorter than its diff:
```python
import functools

import jax
import jax.numpy as jnp
from jax import lax
from jax.experimental import pallas as pl
from jax.experimental.pallas import tpu as pltpu
from jax.sharding import PartitionSpec as P

H = 128
G = 8
HEAD_SIZE = 128
BLOCK = 128
PAGE_TOKENS = 32
NEG = -1e30
F32 = jnp.float32
BF16 = jnp.bfloat16
AXES = ("head", "req", "pd")
CODE = 240.0
PAD_ROWS = 16


def dot(a, b):
    return jnp.dot(a, b, preferred_element_type=F32)


def dot_nt(a, b):
    return lax.dot_general(a, b, (((1,), (1,)), ((), ())), preferred_element_type=F32)


def split2(v):
    high = v.astype(BF16)
    return high, (v - high.astype(F32)).astype(BF16)


def split3(v):
    high = v.astype(BF16)
    rest = v - high.astype(F32)
    middle = rest.astype(BF16)
    return high, middle, (rest - middle.astype(F32)).astype(BF16)


def swap_matrix(rows, cols):
    n = rows * cols
    i = lax.broadcasted_iota(jnp.int32, (n, n), 0)
    j = lax.broadcasted_iota(jnp.int32, (n, n), 1)
    return ((i // rows == j % cols) & (i % rows == j // cols)).astype(F32).astype(BF16)


def token_mask(shape, dim, length, start=0):
    return lax.broadcasted_iota(jnp.int32, shape, dim) + start < length


def state_kernel(sc, x_ref, dt_ref, rate_ref, bt_ref, out_ref, perm, tri, xs, *, hb, part, first):
    r = pl.program_id(0)
    head, block, flip = sc[0], sc[1], sc[2]
    length = sc[4 + first + r]
    span = x_ref.shape[1]
    heads = dt_ref.shape[2]

    @pl.when(r == 0)
    def _():
        perm[...] = swap_matrix(16, hb)
        i = lax.broadcasted_iota(jnp.int32, (span, span), 0)
        j = lax.broadcasted_iota(jnp.int32, (span, span), 1)
        tri[...] = (i > j).astype(F32).astype(BF16)

    dtm = jnp.where(token_mask((span, heads), 0, length), dt_ref[0], 0.0)
    decay = -rate_ref[pl.ds(head, 1), :] * dtm
    decay_t, dtm_t = decay.T, dtm.T
    after = sum(dot(p, tri[...]) for p in split3(decay_t)[::-1])
    tails = jnp.exp(after) * dtm_t
    tail = tails[0:hb]
    for k in range(1, heads // hb):
        tail = jnp.where(block == k, tails[k * hb : (k + 1) * hb], tail)
    for k in range(span // BLOCK):
        lo = k * BLOCK

        @pl.when(lo < length)
        def _():
            for t in range(lo, lo + BLOCK, 16):
                y = dot(perm[...], x_ref[0, t : t + 16].reshape(16 * hb, 128)).astype(BF16)
                for h in range(hb):
                    xs[h, t : t + 16, :] = y[h * 16 : (h + 1) * 16]

        @pl.when(lo >= length)
        def _():
            xs[:, lo : lo + BLOCK, :] = jnp.zeros((hb, BLOCK, 128), BF16)

    bt = bt_ref[0, 0].astype(F32)
    for h in range(hb):
        high, low = split2(bt * tail[h : h + 1])
        st = dot(high, xs[h]) + dot(low, xs[h])
        top = (jnp.max(jnp.abs(st), axis=0, keepdims=True) * 1.01 + 1e-30).astype(BF16)
        level = jnp.abs(st) * (CODE / top.astype(F32)) - CODE / 2
        code = jnp.exp2(level)
        code = jnp.where(st < 0, -code, code).astype(BF16)
        p, local = h // part, h % part
        slot = jnp.bitwise_xor(p, flip)
        out_ref[0, slot, local * 128 : (local + 1) * 128, :] = code
        if local == 0:
            tops = []
        tops.append(top.astype(F32))
        if local == part - 1:
            tops.append(jnp.zeros((PAD_ROWS - part, 128), F32))
            out_ref[0, slot, part * 128 :, :] = jnp.concatenate(tops, axis=0).astype(BF16)


def span_states(sc, x, dt, rate2, bt, hb, part, first, count):
    _, span, heads, width = x.shape
    slots = hb // part
    rows = part * 128 + PAD_ROWS
    return pl.pallas_call(
        functools.partial(state_kernel, hb=hb, part=part, first=first),
        grid_spec=pltpu.PrefetchScalarGridSpec(
            num_scalar_prefetch=1,
            grid=(count,),
            in_specs=[
                pl.BlockSpec((1, span, hb, width), lambda r, s: (r + first, 0, s[1], 0)),
                pl.BlockSpec((1, span, heads), lambda r, s: (r + first, 0, 0)),
                pl.BlockSpec(rate2.shape, lambda r, s: (0, 0)),
                pl.BlockSpec((1, 1, 128, span), lambda r, s: (r + first, s[1], 0, 0)),
            ],
            out_specs=pl.BlockSpec((1, slots, rows, 128), lambda r, s: (r, 0, 0, 0)),
            scratch_shapes=[
                pltpu.VMEM((16 * hb, 16 * hb), BF16),
                pltpu.VMEM((span, span), BF16),
                pltpu.VMEM((hb, span, 128), BF16),
            ],
        ),
        out_shape=jax.ShapeDtypeStruct((count, slots, rows, 128), BF16),
        compiler_params=pltpu.CompilerParams(vmem_limit_bytes=40 << 20),
        cost_estimate=pl.CostEstimate(
            flops=count * hb * 4 * span * 128 * 128,
            bytes_accessed=count * hb * (span + 128) * 256,
            transcendentals=count * hb * 128 * 128,
        ),
        name="span_states",
    )(sc, x, dt, rate2, bt)


def scan_kernel(sc, x_ref, dt_ref, rate_ref, skip_ref, bt_ref, c_ref, out_ref, perm, back, tri, xs, os, state, cols, *, hb, first):
    r = pl.program_id(0)
    block = pl.program_id(1)
    head = sc[0]
    length = sc[4 + first + r]
    span = x_ref.shape[1]
    heads = dt_ref.shape[2]
    count = span // BLOCK

    @pl.when((r == 0) & (block == 0))
    def _():
        perm[...] = swap_matrix(16, hb)
        back[...] = swap_matrix(hb, 16)
        i = lax.broadcasted_iota(jnp.int32, (BLOCK, BLOCK), 0)
        j = lax.broadcasted_iota(jnp.int32, (BLOCK, BLOCK), 1)
        tri[...] = (i >= j).astype(F32).astype(BF16)

    causal = tri[...].astype(F32)
    rates = -rate_ref[pl.ds(head, 1), :]
    skips = skip_ref[pl.ds(head, 1), :]

    def pick(v):
        out = v[:, 0:hb]
        for k in range(1, heads // hb):
            out = jnp.where(block == k, v[:, k * hb : (k + 1) * hb], out)
        return out

    skips = pick(skips)
    for k in range(count):
        lo = k * BLOCK

        @pl.when(lo >= length)
        def _():
            out_ref[0, lo : lo + BLOCK] = jnp.zeros((BLOCK, hb, 128), BF16)

        @pl.when(lo < length)
        def _():
            valid = token_mask((BLOCK, hb), 0, length, lo)
            dt = pick(dt_ref[0, lo : lo + BLOCK])
            dtm = jnp.where(valid, dt, 0.0)
            cum = sum(dot(tri[...], p) for p in split3(pick(rates) * dtm)[::-1])
            level = cum - jnp.where(valid, jnp.log(dt), NEG)
            level_t = level.T
            scores = dot(c_ref[0, 0, lo : lo + BLOCK], bt_ref[0, 0, :, lo : lo + BLOCK]) * causal
            c = c_ref[0, 0, lo : lo + BLOCK]
            cc = jnp.concatenate([c, c], axis=1)
            grown = jnp.exp(cum)
            last = cum[BLOCK - 1 : BLOCK, :]
            last_t = jnp.exp(last)
            bt = bt_ref[0, 0, :, lo : lo + BLOCK].astype(F32)
            total_t = cum.T[:, BLOCK - 1 : BLOCK]
            tail = jnp.exp(total_t - level_t)
            keep = token_mask((BLOCK, 128), 0, length, lo)
            for t in range(0, BLOCK, 16):
                y = dot(perm[...], x_ref[0, lo + t : lo + t + 16].reshape(16 * hb, 128)).astype(BF16)
                for h in range(hb):
                    xs[h, t : t + 16, :] = y[h * 16 : (h + 1) * 16]
            for h in range(hb):
                diff = cum[:, h : h + 1] - level_t[h : h + 1, :]
                weights = jnp.exp(jnp.minimum(diff, 80.0)) * scores
                left = jnp.concatenate(split2(weights), axis=1)
                x = xs[h]
                if k < count - 1:
                    left = jnp.concatenate(
                        [left, jnp.concatenate(split2(bt * tail[h : h + 1]), axis=1)], axis=0
                    )
                both = dot(left, jnp.concatenate([x, x], axis=0))
                out = both[:BLOCK] + skips[:, h : h + 1] * x.astype(F32)
                if k > 0:
                    old = state[h]
                    inter = dot(cc, jnp.concatenate(split2(old), axis=0))
                    out = out + grown[:, h : h + 1] * inter
                if k < count - 1:
                    new = both[BLOCK:]
                    if k > 0:
                        new = new + last_t[:, h : h + 1] * old
                    state[h] = new
                os[h] = jnp.where(keep, out, 0.0).astype(BF16)
            for t in range(0, BLOCK, 16):
                y = dot(back[...], os[:, t : t + 16, :].reshape(hb * 16, 128)).astype(BF16)
                out_ref[0, lo + t : lo + t + 16] = y.reshape(16, hb, 128)


def span_scan(sc, x, dt, rate2, skip2, bt, c, hb, first, count, out):
    reqs, span, heads, width = x.shape
    blocks = heads // hb
    x_spec = pl.BlockSpec((1, span, hb, width), lambda r, b, s: (r + first, 0, b, 0))
    in_specs = [
        x_spec,
        pl.BlockSpec((1, span, heads), lambda r, b, s: (r + first, 0, 0)),
        pl.BlockSpec(rate2.shape, lambda r, b, s: (0, 0)),
        pl.BlockSpec(skip2.shape, lambda r, b, s: (0, 0)),
        pl.BlockSpec((1, 1, 128, span), lambda r, b, s: (r + first, b, 0, 0)),
        pl.BlockSpec((1, 1, span, 128), lambda r, b, s: (r + first, b, 0, 0)),
    ]
    args = [sc, x, dt, rate2, skip2, bt, c]
    body = functools.partial(scan_kernel, hb=hb, first=first)
    aliases = {}
    if out is not None:
        in_specs.append(pl.BlockSpec(memory_space=pl.ANY))
        aliases = {len(args): 0}
        args.append(out)
        inner = body

        def body(*refs):
            return inner(*refs[:7], *refs[8:])

    return pl.pallas_call(
        body,
        grid_spec=pltpu.PrefetchScalarGridSpec(
            num_scalar_prefetch=1,
            grid=(count, blocks),
            in_specs=in_specs,
            out_specs=x_spec,
            scratch_shapes=[
                pltpu.VMEM((16 * hb, 16 * hb), BF16),
                pltpu.VMEM((16 * hb, 16 * hb), BF16),
                pltpu.VMEM((BLOCK, BLOCK), BF16),
                pltpu.VMEM((hb, BLOCK, 128), BF16),
                pltpu.VMEM((hb, BLOCK, 128), BF16),
                pltpu.VMEM((hb, 128, 128), F32),
                pltpu.VMEM((8, 128), F32),
            ],
        ),
        out_shape=jax.ShapeDtypeStruct(x.shape, BF16),
        input_output_aliases=aliases,
        compiler_params=pltpu.CompilerParams(vmem_limit_bytes=40 << 20),
        cost_estimate=pl.CostEstimate(
            flops=count * heads * 16 * span * 128 * 128,
            bytes_accessed=count * heads * span * 512,
            transcendentals=count * heads * span * 128,
        ),
        name="span_scan",
    )(*args)


def page_kernel(sc, table_ref, kv_ref, *refs, dec_reqs, rows):
    count = len(refs) // 2
    head, row0 = sc[0], sc[3]
    reqs, _, pages = kv_ref.shape[:3]
    width = pages * PAGE_TOKENS
    lane = lax.broadcasted_iota(jnp.int32, (1, width), 1)
    for m in range(count):
        q_ref, out_ref = refs[m], refs[count + m]
        split, sub = sc[4 + reqs + 2 * m], sc[5 + reqs + 2 * m]
        kv_local = q_ref.shape[1]
        for i in range(dec_reqs):
            r = sub * dec_reqs + i
            place = jnp.zeros((1, width), jnp.int32)
            for p in range(pages):
                at = table_ref[row0 + r, head * pages + p] * PAGE_TOKENS - p * PAGE_TOKENS
                place = jnp.where(lane // PAGE_TOKENS == p, lane + at, place)
            valid = place < sc[4 + r]
            for v in range(kv_local):
                kv = kv_ref[r, split * kv_local + v]
                keys = kv[:, 0].reshape(width, HEAD_SIZE)
                values = kv[:, 1].reshape(width, HEAD_SIZE)
                s = dot_nt(q_ref[i, v], keys) * (1.0 / HEAD_SIZE**0.5)
                s = jnp.where(valid, s, NEG)
                top = jnp.max(s, axis=1, keepdims=True)
                w = jnp.where(valid, jnp.exp(s - top), 0.0)
                total = jnp.sum(w, axis=1, keepdims=True)
                high, low = split2(w)
                acc = dot(high, values) + dot(low, values)
                out_ref[i, v, 0:rows] = acc / jnp.maximum(total, 1e-30)
                lse = jnp.where(total > 0, top + jnp.log(jnp.maximum(total, 1e-30)), NEG)
                lse_t = jnp.broadcast_to(lse, (rows, HEAD_SIZE)).T[0:8]
                out_ref[i, v, rows:] = jnp.concatenate(
                    [lse_t, jnp.zeros((8, HEAD_SIZE - rows), F32)], axis=1
                )


def page_partials(sc, table, kv, queries, dec_reqs):
    rows = queries[0].shape[2]
    shape = queries[0].shape[:2] + (rows + 8, HEAD_SIZE)
    vmem = pl.BlockSpec(memory_space=pltpu.VMEM)
    return pl.pallas_call(
        functools.partial(page_kernel, dec_reqs=dec_reqs, rows=rows),
        in_specs=[pl.BlockSpec(memory_space=pltpu.SMEM)] * 2 + [vmem] * (1 + len(queries)),
        out_specs=[vmem] * len(queries),
        out_shape=[jax.ShapeDtypeStruct(shape, F32)] * len(queries),
        compiler_params=pltpu.CompilerParams(vmem_limit_bytes=40 << 20),
        cost_estimate=pl.CostEstimate(flops=10**9, bytes_accessed=6 << 20, transcendentals=10**6),
        name="page_partials",
    )(sc, table, kv, *queries)


def merge_kernel(q_ref, kn_ref, *refs, steps):
    parts, out_ref = refs[:-1], refs[-1]
    reqs, kv_local, rows, _ = q_ref.shape
    per_step = rows // steps
    step = lax.broadcasted_iota(jnp.int32, (rows, 1), 0) // per_step
    for r in range(reqs):
        for v in range(kv_local):
            q = q_ref[r, v].astype(F32)
            s = []
            for u in range(steps):
                key = kn_ref[r, v, 0, u : u + 1].astype(F32)
                one = jnp.sum(q * key, axis=1, keepdims=True) * (1.0 / HEAD_SIZE**0.5)
                s.append(jnp.where(step >= u, one, NEG))
            levels = []
            for part in parts:
                lse = part[r, v, rows:]
                levels.append(
                    jnp.concatenate([lse] * (HEAD_SIZE // 8), axis=0).T[0:rows, 0:1]
                )
            top = functools.reduce(jnp.maximum, s + levels)
            total = jnp.zeros((rows, 1), F32)
            acc = jnp.zeros((rows, HEAD_SIZE), F32)
            for u in range(steps):
                w = jnp.where(step >= u, jnp.exp(s[u] - top), 0.0)
                total = total + w
                acc = acc + w * kn_ref[r, v, 1, u : u + 1].astype(F32)
            for part, level in zip(parts, levels):
                w = jnp.exp(level - top)
                total = total + w
                acc = acc + w * part[r, v, 0:rows]
            out_ref[r, v] = (acc / total).astype(BF16)


def merge_partials(q, kv_new, parts, steps):
    vmem = pl.BlockSpec(memory_space=pltpu.VMEM)
    return pl.pallas_call(
        functools.partial(merge_kernel, steps=steps),
        in_specs=[vmem] * (2 + len(parts)),
        out_specs=vmem,
        out_shape=jax.ShapeDtypeStruct(q.shape, BF16),
        compiler_params=pltpu.CompilerParams(vmem_limit_bytes=40 << 20),
        cost_estimate=pl.CostEstimate(flops=10**8, bytes_accessed=2 << 20, transcendentals=10**5),
        name="merge_partials",
    )(q, kv_new, *parts)


def decode_kernel(sc, x_ref, dt_ref, rate_ref, skip_ref, b_ref, c_ref, *refs, count, part):
    messages, (state_ref, out_ref) = refs[:count], refs[-2:]
    split, group_heads = sc[0], H // G
    steps = x_ref.shape[1]
    blocks = x_ref.shape[2]
    b_all = b_ref[0].astype(F32)
    c_all = c_ref[0].astype(F32)
    which = lax.broadcasted_iota(jnp.int32, b_all.shape, 1)
    for m in range(count):
        z = sc[1 + m]
        group = ((z * sc[1 + count] + split) * part) // group_heads
        b = jnp.sum(jnp.where(which == group, b_all, 0.0), axis=1)
        c = jnp.sum(jnp.where(which == group, c_all, 0.0), axis=1)
        pad = jnp.zeros((8 - steps, 128), F32)
        b8 = jnp.concatenate([b, pad], axis=0)
        c8 = jnp.concatenate([c, pad], axis=0)
        gram = dot_nt(c8.astype(BF16), b8.astype(BF16))
        b_t = jnp.concatenate([b8] * 16, axis=0).T
        c16 = jnp.concatenate([c8, pad, c], axis=0)[0:8].astype(BF16)
        cc = jnp.concatenate([c16, c16], axis=1)
        rate = rate_ref[z, split]
        skip = skip_ref[z, split]
        dt = dt_ref[0, z]
        xs = [x_ref[0, j, z].astype(F32) for j in range(steps)]
        cum = []
        for j in range(steps):
            now = -rate * dt[:, j : j + 1]
            cum.append(now if j == 0 else cum[-1] + now)
        fed = [
            jnp.exp(cum[steps - 1] - cum[i]) * dt[:, i : i + 1] * xs[i] for i in range(steps)
        ]
        kept = jnp.broadcast_to(jnp.exp(cum[steps - 1]), (part, 128))
        message = messages[m]
        tops = message[0, part * 128 :, :].astype(F32)
        reads = []
        for h in range(part):
            code = message[0, h * 128 : (h + 1) * 128, :].astype(F32)
            size = (jnp.log2(jnp.abs(code)) + CODE / 2) * (tops[h : h + 1] * (1.0 / CODE))
            old = jnp.where(code < 0, -size, size)
            reads.append(dot(cc, jnp.concatenate(split2(old), axis=0)))
            new = old * kept[h : h + 1]
            for i in range(steps):
                new = new + b_t[:, i : i + 1] * fed[i][h : h + 1]
            state_ref[0, z, h] = new.T
        for j in range(steps):
            read = jnp.concatenate([one[j : j + 1] for one in reads], axis=0)
            out = jnp.exp(cum[j]) * read + skip * xs[j]
            for i in range(j + 1):
                out = out + (jnp.exp(cum[j] - cum[i]) * dt[:, i : i + 1] * gram[j : j + 1, i : i + 1]) * xs[i]
            out_ref[0, j, z] = out.astype(BF16)


def decode(sc, x, dt_t, rate4, skip4, b, c, messages, first, outs):
    reqs, steps, blocks, part, width = x.shape
    count = len(messages)
    step = messages[0].shape[0]
    per_req = lambda shape: pl.BlockSpec(
        (1,) + shape[1:], lambda r, s: (r + first,) + (0,) * (len(shape) - 1)
    )
    whole = lambda a: pl.BlockSpec(a.shape, lambda r, s: (0,) * a.ndim)
    in_specs = [per_req(x.shape), per_req(dt_t.shape), whole(rate4), whole(skip4), per_req(b.shape), per_req(c.shape)]
    in_specs += [pl.BlockSpec((1,) + m.shape[1:], lambda r, s: (r, 0, 0)) for m in messages]
    args = [sc, x, dt_t, rate4, skip4, b, c, *messages]
    aliases = {}
    if outs is not None:
        aliases = {len(args): 0, len(args) + 1: 1}
        in_specs += [pl.BlockSpec(memory_space=pl.ANY)] * 2
        args += list(outs)
    state_shape = (reqs, blocks, part, 128, 128)
    return pl.pallas_call(
        functools.partial(decode_kernel, count=count, part=part),
        grid_spec=pltpu.PrefetchScalarGridSpec(
            num_scalar_prefetch=1,
            grid=(step,),
            in_specs=in_specs,
            out_specs=[per_req(state_shape), per_req(x.shape)],
        ),
        out_shape=[jax.ShapeDtypeStruct(state_shape, F32), jax.ShapeDtypeStruct(x.shape, BF16)],
        input_output_aliases=aliases,
        compiler_params=pltpu.CompilerParams(vmem_limit_bytes=40 << 20),
        cost_estimate=pl.CostEstimate(
            flops=step * blocks * part * 128 * 128 * 16,
            bytes_accessed=step * blocks * part * 128 * 128 * 6,
            transcendentals=step * blocks * part * 128 * 128,
        ),
        name="decode_steps",
    )(*args)


def local(
    x_pre,
    dt_pre,
    b_pre,
    c_pre,
    rate,
    skip,
    lengths,
    table,
    kv_pages,
    query,
    kv_new,
    x_dec,
    dt_dec,
    b_dec,
    c_dec,
):
    n_head, n_req, n_pd = (lax.axis_size(a) for a in AXES)
    n_split = n_req * n_pd
    ratio = n_head // n_split
    head, req, pd = (lax.axis_index(a) for a in AXES)
    split = req * n_pd + pd
    reqs, span, heads, _ = x_pre.shape
    part = heads // n_split
    dec_reqs, steps, kv_local, query_width = query.shape
    hb = min(heads, H // G)
    blocks = heads // hb
    head_x, head_c, head_q = head // (n_pd * ratio), (head // ratio) % n_pd, head % ratio
    xor = jnp.bitwise_xor

    def index(h, x, c):
        return (h * n_req + x) * n_pd + c

    def places():
        return [(h, x, c) for h in range(n_head) for x in range(n_req) for c in range(n_pd)]

    groups = max(heads // (H // G), 1)
    group0 = (head * heads) // (H // G)
    b_own = lax.dynamic_slice_in_dim(b_pre, group0, groups, 2)
    c_own = lax.dynamic_slice_in_dim(c_pre, group0, groups, 2)
    bt = jnp.transpose(b_own, (0, 2, 3, 1))
    ct = jnp.transpose(c_own, (0, 2, 1, 3))
    rate2, skip2 = rate.reshape(n_head, heads), skip.reshape(n_head, heads)
    row0 = split * reqs
    own = lax.dynamic_slice_in_dim(lengths, row0, reqs, 0)

    def scalars(block, extra=()):
        first = jnp.stack([head, block, head_c, row0]).astype(jnp.int32)
        more = [jnp.stack(extra).astype(jnp.int32)] if extra else []
        return jnp.concatenate([first, own] + more)

    group_q = query_width // HEAD_SIZE
    q = query.reshape(dec_reqs, steps, kv_local, group_q, HEAD_SIZE)
    q = jnp.transpose(q, (0, 2, 1, 3, 4)).reshape(dec_reqs, kv_local, steps * group_q, HEAD_SIZE)
    sent, origin, routes = [], [], []
    for k in range(n_split):
        for i in range(ratio):
            route = []
            for h, x, c in places():
                to_split = h // ratio
                to_head = ((x * n_pd + c) ^ k) * ratio + ((h % ratio) ^ i)
                route.append((index(h, x, c), index(to_head, to_split // n_pd, to_split % n_pd)))
            sent.append(lax.ppermute(q, AXES, route))
            origin += [xor(head // ratio, k), xor(head % ratio, i)]
            routes.append([(b, a) for a, b in route])

    chunks = dec_reqs if ratio == 1 else 1
    size = reqs // chunks
    per_plane = heads // n_req
    mixed = []
    own_parts = []
    for chunk in range(chunks):
        if per_plane == hb:
            parts = [
                span_states(scalars(xor(req, j)), x_pre, dt_pre, rate2, bt, hb, part, chunk * size, size)
                for j in reversed(range(n_req))
            ][::-1]
        else:
            whole = span_states(scalars(jnp.int32(0)), x_pre, dt_pre, rate2, bt, hb, part, chunk * size, size)
            parts = [lax.dynamic_slice_in_dim(whole, xor(req, j) * n_pd, n_pd, 1) for j in range(n_req)]
        arrived = [parts[0]]
        for j in range(1, n_req):
            route = [(index(h, x, c), index(h, x ^ j, c)) for h, x, c in places()]
            arrived.append(lax.ppermute(parts[j], AXES, route))
        mixed.append(arrived)

    page_sums = page_partials(scalars(jnp.int32(0), origin), table, kv_pages, sent, dec_reqs)
    returned = [lax.ppermute(a, AXES, route) for a, route in zip(page_sums, routes)]

    rate4 = rate.reshape(n_head, n_split, part, 1)
    skip4 = skip.reshape(n_head, n_split, part, 1)
    dt_t = jnp.transpose(dt_dec, (0, 2, 3, 1))
    outs = None
    prefill = None
    for chunk in range(chunks):
        messages, sources = [], []
        for kj in range(n_req):
            from_x = xor(xor(head_x, req), kj)
            payload = mixed[chunk][0]
            for j in range(1, n_req):
                payload = jnp.where(from_x == j, mixed[chunk][j], payload)
            for kc in range(n_pd):
                for ki in range(ratio):
                    route = []
                    for h, x, c in places():
                        hx, hc, hq = h // (n_pd * ratio), (h // ratio) % n_pd, h % ratio
                        to = ((hx ^ kj) * n_pd + c) * ratio + (hq ^ ki)
                        route.append((index(h, x, c), index(to, x, hc ^ kc)))
                    piece = lax.dynamic_slice_in_dim(
                        payload[:, kc], xor(head_q, ki) * (size // ratio), size // ratio, 0
                    )
                    messages.append(lax.ppermute(piece, AXES, route))
                    sources.append((xor(head_x, kj) * n_pd + xor(pd, kc)) * ratio + xor(head_q, ki))
        sc = jnp.stack([split] + sources + [jnp.int32(n_split)]).astype(jnp.int32)
        prefill = span_scan(scalars(jnp.int32(0)), x_pre, dt_pre, rate2, skip2, bt, ct, hb, chunk * size, size, prefill)
        outs = decode(sc, x_dec, dt_t, rate4, skip4, b_dec, c_dec, messages, chunk * (dec_reqs // chunks), outs)
    decode_state, decode_out = outs

    news = jnp.transpose(kv_new, (0, 2, 3, 1, 4))
    attn = merge_partials(q, news, returned, steps)
    attn = attn.reshape(dec_reqs, kv_local, steps, group_q, HEAD_SIZE)
    attn_out = jnp.transpose(attn, (0, 2, 1, 3, 4)).reshape(query.shape)
    return (prefill, decode_out, decode_state, attn_out)


def solution(mesh):
    placed = (
        P(("group", "req", "pd"), None, "head", None),
        P(("group", "req", "pd"), None, "head"),
        P(("group", "req", "pd"), None, None, None),
        P(("group", "req", "pd"), None, None, None),
        P(),
        P(),
        P("group"),
        P("group", None),
        P(("group", "req", "pd"), None, "head", None, None, None),
        P(("group", "head"), None, ("req", "pd"), None),
        P(("group", "head"), None, ("req", "pd"), None, None),
        P(("group", "head"), None, None, ("req", "pd"), None),
        P(("group", "head"), None, None, ("req", "pd")),
        P(("group", "head"), None, None, None),
        P(("group", "head"), None, None, None),
    )
    return jax.shard_map(
        local,
        mesh=mesh,
        in_specs=placed,
        out_specs=(
            P(("group", "req", "pd"), None, "head", None),
            P(("group", "head"), None, None, ("req", "pd"), None),
            P(("group", "head"), None, ("req", "pd"), None, None),
            P(("group", "head"), None, ("req", "pd"), None),
        ),
        check_vma=False,
    )
```

time: 775 us -> 308 us (0.40)
  the two profiles are of different devices: /device:TPU:0 before, /device:TPU:18 now
where the time goes in v1:
time: 308 us; the launch traced here: 312 us
  Pallas kernels  124 us (40%)
  waiting for transfers between devices  83.9 us (27%)
  starting transfers between devices  70.7 us (23%)
  local copies, waits for them, and re-layouts  30 us (10%)
    ppermute x16, waiting for transfers between devices, local(): messages.append(lax.ppermute(piece, AXES, route))  53.9 us
    pallas_call x8, Pallas kernels, span_states(): pl.pallas_call(functools.partial(state_kernel, hb=hb, part=part, first=fi...  52.4 us
    pallas_call x4, Pallas kernels, span_scan(): pl.pallas_call(body, grid_spec=pltpu.PrefetchScalarGridSpec(num_scalar_pr...  49.5 us
    ppermute x16, starting transfers between devices, local(): messages.append(lax.ppermute(piece, AXES, route))  32.1 us
    ppermute x4, waiting for transfers between devices, local(): arrived.append(lax.ppermute(parts[j], AXES, route))  30.1 us
    ppermute x4, starting transfers between devices, local(): arrived.append(lax.ppermute(parts[j], AXES, route))  26.2 us
    pallas_call x4, Pallas kernels, decode(): pl.pallas_call(functools.partial(decode_kernel, count=count, part=part),...  18.5 us
    unnamed x97, local copies, waits for them, and re-layouts  16.7 us
  transfers between devices with their start and end apart: 28, of which 10 were waited for; matrix products, arithmetic and copies ran while one was open for 6% of the time, Pallas kernels for 38%

profile of v1, /device:TPU:18, one launch (start us, length us, event | category | flops | bytes accessed | tf_op | source)
XLA Modules:
  0.0 311.6 jit_solution(2479246171697976940)
XLA Ops:
  5.1 2.9 collective-permute-start.22
  10.1 6.6 %constant_dynamic-slice_fusion = (bf16[4,512,2,128]{3,2,1,0:T(2,128)(2,1)}, bf16[4,512,2,128]{3,2,1,0:T(2,128)(2,1)S(1)}) fusion(bf16[4,512,8,128]{3,2,1,0:T(8,128)(2,1)} %param.18, s32[]{:T(128)S(6)} %select_n.93, bf16[4,512,8,128]{3,2,1,0:T(8,128)(2,1)} %param.17), kind=kLoop, calls=%fused_computation.27 | loop fusion | bytes 4194308 | tf_op jit(solution)/shard_map/dynamic_slice | solution.py:503
  18.3 6.4 %span_states.8 = bf16[1,2,1040,128]{3,2,1,0:T(8,128)(2,1)} custom-call(s32[8]{0:T(128)S(1)} %concatenate.9.sc, bf16[4,512,32,128]{3,2,1,0:T(8,128)(2,1)} %x_ref.21, f32[4,512,32]{2,1,0:T(8,128)S(1)} %copy.33.dt_ref.refs_2_, f32[4,32]{1,0:T(4,128)S(1)} %reshape.32.rate_ref.refs_3_, bf16[4,2,128,512]{3,2,1,0:T(8,128)(2,1)S(1)} %bitcast.65), custom_call_target="tpu_custom_call" | custom-call | flops 536870912 | bytes 2621440 | tf_op jit(solution)/shard_map/span_states/pallas_call | solution.py:113
  26.3 4.9 %span_states.10 = bf16[1,2,1040,128]{3,2,1,0:T(8,128)(2,1)S(1)} custom-call(s32[8]{0:T(128)S(1)} %concatenate.9.sc, bf16[4,512,32,128]{3,2,1,0:T(8,128)(2,1)} %x_ref.21, f32[4,512,32]{2,1,0:T(8,128)S(1)} %copy.33.dt_ref.refs_2_, f32[4,32]{1,0:T(4,128)S(1)} %reshape.32.rate_ref.refs_3_, bf16[4,2,128,512]{3,2,1,0:T(8,128)(2,1)S(1)} %bitcast.66), custom_call_target="tpu_custom_call" | custom-call | flops 536870912 | bytes 2621440 | tf_op jit(solution)/shard_map/span_states/pallas_call | solution.py:113
  32.0 5.8 %span_states.9 = bf16[1,2,1040,128]{3,2,1,0:T(8,128)(2,1)S(1)} custom-call(s32[8]{0:T(128)S(1)} %concatenate.10.sc, bf16[4,512,32,128]{3,2,1,0:T(8,128)(2,1)} %x_ref.21, f32[4,512,32]{2,1,0:T(8,128)S(1)} %copy.33.dt_ref.refs_2_, f32[4,32]{1,0:T(4,128)S(1)} %reshape.32.rate_ref.refs_3_, bf16[4,2,128,512]{3,2,1,0:T(8,128)(2,1)S(1)} %bitcast.67), custom_call_target="tpu_custom_call" | custom-call | flops 536870912 | bytes 2621440 | tf_op jit(solution)/shard_map/span_states/pallas_call | solution.py:113
  38.7 4.9 %span_states.11 = bf16[1,2,1040,128]{3,2,1,0:T(8,128)(2,1)S(1)} custom-call(s32[8]{0:T(128)S(1)} %concatenate.10.sc, bf16[4,512,32,128]{3,2,1,0:T(8,128)(2,1)} %x_ref.21, f32[4,512,32]{2,1,0:T(8,128)S(1)} %copy.33.dt_ref.refs_2_, f32[4,32]{1,0:T(4,128)S(1)} %reshape.32.rate_ref.refs_3_, bf16[4,2,128,512]{3,2,1,0:T(8,128)(2,1)S(1)} %bitcast.68), custom_call_target="tpu_custom_call" | custom-call | flops 536870912 | bytes 2621440 | tf_op jit(solution)/shard_map/span_states/pallas_call | solution.py:113
  44.4 4.9 %span_states.12 = bf16[1,2,1040,128]{3,2,1,0:T(8,128)(2,1)S(1)} custom-call(s32[8]{0:T(128)S(1)} %concatenate.9.sc, bf16[4,512,32,128]{3,2,1,0:T(8,128)(2,1)} %x_ref.21, f32[4,512,32]{2,1,0:T(8,128)S(1)} %copy.33.dt_ref.refs_2_, f32[4,32]{1,0:T(4,128)S(1)} %reshape.32.rate_ref.refs_3_, bf16[4,2,128,512]{3,2,1,0:T(8,128)(2,1)S(1)} %bitcast.69), custom_call_target="tpu_custom_call" | custom-call | flops 536870912 | bytes 2621440 | tf_op jit(solution)/shard_map/span_states/pallas_call | solution.py:113
  50.0 15.8 %span_states.13 = bf16[1,2,1040,128]{3,2,1,0:T(8,128)(2,1)S(1)} custom-call(s32[8]{0:T(128)S(1)} %concatenate.10.sc, bf16[4,512,32,128]{3,2,1,0:T(8,128)(2,1)} %x_ref.21, f32[4,512,32]{2,1,0:T(8,128)S(1)} %copy.33.dt_ref.refs_2_, f32[4,32]{1,0:T(4,128)S(1)} %reshape.32.rate_ref.refs_3_, bf16[4,2,128,512]{3,2,1,0:T(8,128)(2,1)S(1)} %bitcast.70), custom_call_target="tpu_custom_call" | custom-call | flops 536870912 | bytes 2621440 | tf_op jit(solution)/shard_map/span_states/pallas_call | solution.py:113
  68.2 7.5 %span_scan.4.refs_7_ = bf16[4,512,32,128]{3,2,1,0:T(8,128)(2,1)} custom-call(s32[8]{0:T(128)S(1)} %concatenate.8.sc.refs_0_, bf16[4,512,32,128]{3,2,1,0:T(8,128)(2,1)} %x_ref.21, f32[4,512,32]{2,1,0:T(8,128)S(1)} %copy.33.dt_ref.refs_2_, f32[4,32]{1,0:T(4,128)S(1)} %reshape.32.rate_ref.refs_3_, f32[4,32]{1,0:T(4,128)S(1)} %reshape.33.skip_ref.refs_4_, ...), custom_call_target="tpu_custom_call" | custom-call | flops 4294967296 | bytes 8388608 | tf_op jit(solution)/shard_map/span_scan/pallas_call | solution.py:249
  75.7 11.4 %span_scan.5.refs_7_ = bf16[4,512,32,128]{3,2,1,0:T(8,128)(2,1)} custom-call(s32[8]{0:T(128)S(1)} %concatenate.8.sc.refs_0_, bf16[4,512,32,128]{3,2,1,0:T(8,128)(2,1)} %x_ref.21, f32[4,512,32]{2,1,0:T(8,128)S(1)} %copy.33.dt_ref.refs_2_, f32[4,32]{1,0:T(4,128)S(1)} %reshape.32.rate_ref.refs_3_, ...), custom_call_target="tpu_custom_call", output_to_operand_aliasing={{}: (7, {})} | custom-call | flops 4294967296 | bytes 8388608 | tf_op jit(solution)/shard_map/span_scan/pallas_call | solution.py:249
  87.1 11.6 %span_scan.6.refs_7_ = bf16[4,512,32,128]{3,2,1,0:T(8,128)(2,1)} custom-call(s32[8]{0:T(128)S(1)} %concatenate.8.sc.refs_0_, bf16[4,512,32,128]{3,2,1,0:T(8,128)(2,1)} %x_ref.21, f32[4,512,32]{2,1,0:T(8,128)S(1)} %copy.33.dt_ref.refs_2_, f32[4,32]{1,0:T(4,128)S(1)} %reshape.32.rate_ref.refs_3_, ...), custom_call_target="tpu_custom_call", output_to_operand_aliasing={{}: (7, {})} | custom-call | flops 4294967296 | bytes 8388608 | tf_op jit(solution)/shard_map/span_scan/pallas_call | solution.py:249
  98.8 4.5 %span_states.14 = bf16[1,2,1040,128]{3,2,1,0:T(8,128)(2,1)S(1)} custom-call(s32[8]{0:T(128)S(1)} %concatenate.9.sc, bf16[4,512,32,128]{3,2,1,0:T(8,128)(2,1)} %x_ref.21, f32[4,512,32]{2,1,0:T(8,128)S(1)} %copy.33.dt_ref.refs_2_, f32[4,32]{1,0:T(4,128)S(1)} %reshape.32.rate_ref.refs_3_, bf16[4,2,128,512]{3,2,1,0:T(8,128)(2,1)S(1)} %bitcast.74), custom_call_target="tpu_custom_call" | custom-call | flops 536870912 | bytes 2621440 | tf_op jit(solution)/shard_map/span_states/pallas_call | solution.py:113
  105.6 5.2 %span_states.15 = bf16[1,2,1040,128]{3,2,1,0:T(8,128)(2,1)S(1)} custom-call(s32[8]{0:T(128)S(1)} %concatenate.10.sc, bf16[4,512,32,128]{3,2,1,0:T(8,128)(2,1)} %x_ref.21, f32[4,512,32]{2,1,0:T(8,128)S(1)} %copy.33.dt_ref.refs_2_, f32[4,32]{1,0:T(4,128)S(1)} %reshape.32.rate_ref.refs_3_, bf16[4,2,128,512]{3,2,1,0:T(8,128)(2,1)S(1)} %bitcast.75), custom_call_target="tpu_custom_call" | custom-call | flops 536870912 | bytes 2621440 | tf_op jit(solution)/shard_map/span_states/pallas_call | solution.py:113
  110.8 22.6 %collective-permute-start.5 = (bf16[1,2,1040,128]{3,2,1,0:T(8,128)(2,1)S(1)}, bf16[1,2,1040,128]{3,2,1,0:T(8,128)(2,1)S(1)}, u32[]{:S(2)}, u32[]{:S(2)}) collective-permute-start(bf16[1,2,1040,128]{3,2,1,0:T(8,128)(2,1)S(1)} %copy-done.12), channel_id=1, source_target_pairs={{0,2},{1,3},{2,0},{3,1},{4,6},{5,7},{6,4},{7,5},{8,10},{9,11},{10,... | collective-permute-start | bytes 1597448 | tf_op jit(solution)/shard_map/ppermute | solution.py:547
  142.9 4.8 %collective-permute-done.5 = bf16[1,2,1040,128]{3,2,1,0:T(8,128)(2,1)S(1)} collective-permute-done((bf16[1,2,1040,128]{3,2,1,0:T(8,128)(2,1)S(1)}, bf16[1,2,1040,128]{3,2,1,0:T(8,128)(2,1)S(1)}, u32[]{:S(2)}, u32[]{:S(2)}) %collective-permute-start.5) | collective-permute-done | bytes 532512 | tf_op jit(solution)/shard_map/ppermute | solution.py:547
  147.7 3.0 collective-permute-start.26
  151.6 14.6 %collective-permute-done.10 = bf16[1,2,1040,128]{3,2,1,0:T(8,128)(2,1)S(1)} collective-permute-done((bf16[1,2,1040,128]{3,2,1,0:T(8,128)(2,1)S(1)}, bf16[1,2,1040,128]{3,2,1,0:T(8,128)(2,1)S(1)}, u32[]{:S(2)}, u32[]{:S(2)}) %collective-permute-start.10) | collective-permute-done | bytes 532512 | tf_op jit(solution)/shard_map/ppermute | solution.py:547
  166.3 10.8 %collective-permute-done.15 = bf16[1,2,1040,128]{3,2,1,0:T(8,128)(2,1)S(1)} collective-permute-done((bf16[1,2,1040,128]{3,2,1,0:T(8,128)(2,1)S(1)}, bf16[1,2,1040,128]{3,2,1,0:T(8,128)(2,1)S(1)}, u32[]{:S(2)}, u32[]{:S(2)}) %collective-permute-start.15) | collective-permute-done | bytes 532512 | tf_op jit(solution)/shard_map/ppermute | solution.py:547
  177.9 4.5 %collective-permute-start.7 = (bf16[1,1040,128]{2,1,0:T(8,128)(2,1)S(1)}, bf16[1,1040,128]{2,1,0:T(8,128)(2,1)S(1)}, u32[]{:S(2)}, u32[]{:S(2)}) collective-permute-start(bf16[1,1040,128]{2,1,0:T(8,128)(2,1)S(1)} %get-tuple-element.46), channel_id=1, source_target_pairs={{0,1},{1,5},{2,3},{3,7},{4,0},{5,4},{6,2},{7,6},{8,9},{9,13},{10,1... | collective-permute-start | bytes 798728 | tf_op jit(solution)/shard_map/ppermute | solution.py:575
  182.3 4.0 %collective-permute-start.8 = (bf16[1,1040,128]{2,1,0:T(8,128)(2,1)S(1)}, bf16[1,1040,128]{2,1,0:T(8,128)(2,1)S(1)}, u32[]{:S(2)}, u32[]{:S(2)}) collective-permute-start(bf16[1,1040,128]{2,1,0:T(8,128)(2,1)S(1)} %get-tuple-element.45), channel_id=1, source_target_pairs={{0,8},{1,12},{2,10},{3,14},{4,9},{5,13},{6,11},{7,15},{8,0},{9,4},... | collective-permute-start | bytes 798728 | tf_op jit(solution)/shard_map/ppermute | solution.py:575
  191.1 5.1 %collective-permute-start.14 = (bf16[1,1040,128]{2,1,0:T(8,128)(2,1)S(1)}, bf16[1,1040,128]{2,1,0:T(8,128)(2,1)S(1)}, u32[]{:S(2)}, u32[]{:S(2)}) collective-permute-start(bf16[1,1040,128]{2,1,0:T(8,128)(2,1)S(1)} %get-tuple-element.40), channel_id=1, source_target_pairs={{0,9},{1,13},{2,11},{3,15},{4,8},{5,12},{6,10},{7,14},{8,1},{9,5},... | collective-permute-start | bytes 798728 | tf_op jit(solution)/shard_map/ppermute | solution.py:575
  196.2 7.7 %collective-permute-done.8.refs_2_ = bf16[1,1040,128]{2,1,0:T(8,128)(2,1)S(1)} collective-permute-done((bf16[1,1040,128]{2,1,0:T(8,128)(2,1)S(1)}, bf16[1,1040,128]{2,1,0:T(8,128)(2,1)S(1)}, u32[]{:S(2)}, u32[]{:S(2)}) %collective-permute-start.8) | collective-permute-done | bytes 266272 | tf_op jit(solution)/shard_map/ppermute | solution.py:575
  208.4 10.6 %collective-permute-done.13.refs_2_ = bf16[1,1040,128]{2,1,0:T(8,128)(2,1)S(1)} collective-permute-done((bf16[1,1040,128]{2,1,0:T(8,128)(2,1)S(1)}, bf16[1,1040,128]{2,1,0:T(8,128)(2,1)S(1)}, u32[]{:S(2)}, u32[]{:S(2)}) %collective-permute-start.13) | collective-permute-done | bytes 266272 | tf_op jit(solution)/shard_map/ppermute | solution.py:575
  219.8 12.8 %collective-permute-done.14.refs_3_ = bf16[1,1040,128]{2,1,0:T(8,128)(2,1)S(1)} collective-permute-done((bf16[1,1040,128]{2,1,0:T(8,128)(2,1)S(1)}, bf16[1,1040,128]{2,1,0:T(8,128)(2,1)S(1)}, u32[]{:S(2)}, u32[]{:S(2)}) %collective-permute-start.14) | collective-permute-done | bytes 266272 | tf_op jit(solution)/shard_map/ppermute | solution.py:575
  232.6 3.6 %collective-permute-start.1 = (bf16[1,1040,128]{2,1,0:T(8,128)(2,1)}, bf16[1,1040,128]{2,1,0:T(8,128)(2,1)}, u32[]{:S(2)}, u32[]{:S(2)}) collective-permute-start(bf16[1,1040,128]{2,1,0:T(8,128)(2,1)} %get-tuple-element.51), channel_id=1, source_target_pairs={{0,0},{1,4},{2,2},{3,6},{4,1},{5,5},{6,3},{7,7},{8,8},{9,12},{10,1... | collective-permute-start | bytes 798728 | tf_op jit(solution)/shard_map/ppermute | solution.py:575
  240.4 20.7 %collective-permute-done.19.refs_3_ = bf16[1,1040,128]{2,1,0:T(8,128)(2,1)S(1)} collective-permute-done((bf16[1,1040,128]{2,1,0:T(8,128)(2,1)S(1)}, bf16[1,1040,128]{2,1,0:T(8,128)(2,1)S(1)}, u32[]{:S(2)}, u32[]{:S(2)}) %collective-permute-start.19) | collective-permute-done | bytes 266272 | tf_op jit(solution)/shard_map/ppermute | solution.py:575
  261.2 3.0 collective-permute-start.9
  264.2 19.0 %span_scan.7 = bf16[4,512,32,128]{3,2,1,0:T(8,128)(2,1)} custom-call(s32[8]{0:T(128)S(1)} %concatenate.8.sc.refs_0_, bf16[4,512,32,128]{3,2,1,0:T(8,128)(2,1)} %x_ref.21, f32[4,512,32]{2,1,0:T(8,128)S(1)} %copy.33.dt_ref.refs_2_, f32[4,32]{1,0:T(4,128)S(1)} %reshape.32.rate_ref.refs_3_, ...), custom_call_target="tpu_custom_call", output_to_operand_aliasing={{}: (7, {})} | custom-call | flops 4294967296 | bytes 8388608 | tf_op jit(solution)/shard_map/span_scan/pallas_call | solution.py:249
  289.0 4.1 %decode_steps.4 = (f32[4,4,8,128,128]{4,3,2,1,0:T(8,128)}, bf16[4,4,4,8,128]{4,3,2,1,0:T(8,128)(2,1)}) custom-call(s32[6]{0:T(128)S(1)} %stack.36.sc, bf16[4,4,4,8,128]{4,3,2,1,0:T(8,128)(2,1)S(1)} %copy-done.6, f32[4,4,8,4]{3,2,1,0:T(8,128)S(1)} %bitcast.81, f32[4,4,8,1]{3,2,1,0:T(8,128)S(1)} %reshape.40.rate_ref, f32[4,4,8,1]{3,2,1,0:T(8,128)S(1)} %reshape.41.skip_ref, ...), custom_call_target="tpu_custom_call" | custom-call | flops 8388608 | bytes 3145728 | tf_op jit(solution)/shard_map/decode_steps/pallas_call | solution.py:444
  296.9 4.1 %decode_steps.5 = (f32[4,4,8,128,128]{4,3,2,1,0:T(8,128)}, bf16[4,4,4,8,128]{4,3,2,1,0:T(8,128)(2,1)}) custom-call(s32[6]{0:T(128)S(1)} %stack.36.sc, bf16[4,4,4,8,128]{4,3,2,1,0:T(8,128)(2,1)S(1)} %copy-done.6, f32[4,4,8,4]{3,2,1,0:T(8,128)S(1)} %bitcast.82, f32[4,4,8,1]{3,2,1,0:T(8,128)S(1)} %reshape.40.rate_ref, ...), custom_call_target="tpu_custom_call", output_to_operand_aliasing={{0}: (11, {}), {1}: (12, {})} | custom-call | flops 8388608 | bytes 3145728 | tf_op jit(solution)/shard_map/decode_steps/pallas_call | solution.py:444
  301.0 5.0 %decode_steps.6 = (f32[4,4,8,128,128]{4,3,2,1,0:T(8,128)}, bf16[4,4,4,8,128]{4,3,2,1,0:T(8,128)(2,1)}) custom-call(s32[6]{0:T(128)S(1)} %stack.36.sc, bf16[4,4,4,8,128]{4,3,2,1,0:T(8,128)(2,1)S(1)} %copy-done.6, f32[4,4,8,4]{3,2,1,0:T(8,128)S(1)} %bitcast.83, f32[4,4,8,1]{3,2,1,0:T(8,128)S(1)} %reshape.40.rate_ref, ...), custom_call_target="tpu_custom_call", output_to_operand_aliasing={{0}: (11, {}), {1}: (12, {})} | custom-call | flops 8388608 | bytes 3145728 | tf_op jit(solution)/shard_map/decode_steps/pallas_call | solution.py:444
  306.1 5.3 %decode_steps.7 = (f32[4,4,8,128,128]{4,3,2,1,0:T(8,128)}, bf16[4,4,4,8,128]{4,3,2,1,0:T(8,128)(2,1)}) custom-call(s32[6]{0:T(128)S(1)} %stack.36.sc, bf16[4,4,4,8,128]{4,3,2,1,0:T(8,128)(2,1)S(1)} %copy-done.6, f32[4,4,8,4]{3,2,1,0:T(8,128)S(1)} %bitcast.84, f32[4,4,8,1]{3,2,1,0:T(8,128)S(1)} %reshape.40.rate_ref, ...), custom_call_target="tpu_custom_call", output_to_operand_aliasing={{0}: (11, {}), {1}: (12, {})} | custom-call | flops 8388608 | bytes 3145728 | tf_op jit(solution)/shard_map/decode_steps/pallas_call | solution.py:444
  (166 shorter events, 52.4 us)
Async XLA Ops:
  1.6 109.2 %collective-permute-start.20 = (bf16[4,2,32,128]{3,2,1,0:T(8,128)(2,1)S(1)}, bf16[4,2,32,128]{3,2,1,0:T(8,128)(2,1)S(1)}, u32[]{:S(2)}, u32[]{:S(2)}) collective-permute-start(bf16[4,2,32,128]{3,2,1,0:T(8,128)(2,1)S(1)} %bitcast.85), channel_id=1, source_target_pairs={{0,0},{1,4},{2,8},{3,12},{4,1},{5,5},{6,9},{7,13},{8,2},{9,6},{10,... | collective-permute-start | bytes 196616 | tf_op jit(solution)/shard_map/ppermute | solution.py:526
  2.2 131.2 %collective-permute-start.21 = (bf16[4,2,32,128]{3,2,1,0:T(8,128)(2,1)S(1)}, bf16[4,2,32,128]{3,2,1,0:T(8,128)(2,1)}, u32[]{:S(2)}, u32[]{:S(2)}) collective-permute-start(bf16[4,2,32,128]{3,2,1,0:T(8,128)(2,1)S(1)} %bitcast.86), channel_id=1, source_target_pairs={{0,4},{1,0},{2,12},{3,8},{4,5},{5,1},{6,13},{7,9},{8,6},{9,2},{10,... | collective-permute-start | bytes 196616 | tf_op jit(solution)/shard_map/ppermute | solution.py:526
  5.1 128.3 %collective-permute-start.22 = (bf16[4,2,32,128]{3,2,1,0:T(8,128)(2,1)S(1)}, bf16[4,2,32,128]{3,2,1,0:T(8,128)(2,1)}, u32[]{:S(2)}, u32[]{:S(2)}) collective-permute-start(bf16[4,2,32,128]{3,2,1,0:T(8,128)(2,1)S(1)} %bitcast.87), channel_id=1, source_target_pairs={{0,8},{1,12},{2,0},{3,4},{4,9},{5,13},{6,1},{7,5},{8,10},{9,14},{1... | collective-permute-start | bytes 196616 | tf_op jit(solution)/shard_map/ppermute | solution.py:526
  8.0 127.4 %collective-permute-start.23 = (bf16[4,2,32,128]{3,2,1,0:T(8,128)(2,1)S(1)}, bf16[4,2,32,128]{3,2,1,0:T(8,128)(2,1)}, u32[]{:S(2)}, u32[]{:S(2)}) collective-permute-start(bf16[4,2,32,128]{3,2,1,0:T(8,128)(2,1)S(1)} %bitcast.88), channel_id=1, source_target_pairs={{0,12},{1,8},{2,4},{3,0},{4,13},{5,9},{6,5},{7,1},{8,14},{9,10},{1... | collective-permute-start | bytes 196616 | tf_op jit(solution)/shard_map/ppermute | solution.py:526
  24.7 114.1 %collective-permute-start = (bf16[1,2,1040,128]{3,2,1,0:T(8,128)(2,1)}, bf16[1,2,1040,128]{3,2,1,0:T(8,128)(2,1)}, u32[]{:S(2)}, u32[]{:S(2)}) collective-permute-start(bf16[1,2,1040,128]{3,2,1,0:T(8,128)(2,1)} %span_states.8), channel_id=1, source_target_pairs={{0,2},{1,3},{2,0},{3,1},{4,6},{5,7},{6,4},{7,5},{8,10},{9,11},{10,... | collective-permute-start | bytes 1597448 | tf_op jit(solution)/shard_map/ppermute | solution.py:547
  110.8 36.9 %collective-permute-start.5 = (bf16[1,2,1040,128]{3,2,1,0:T(8,128)(2,1)S(1)}, bf16[1,2,1040,128]{3,2,1,0:T(8,128)(2,1)S(1)}, u32[]{:S(2)}, u32[]{:S(2)}) collective-permute-start(bf16[1,2,1040,128]{3,2,1,0:T(8,128)(2,1)S(1)} %copy-done.12), channel_id=1, source_target_pairs={{0,2},{1,3},{2,0},{3,1},{4,6},{5,7},{6,4},{7,5},{8,10},{9,11},{10,... | collective-permute-start | bytes 1597448 | tf_op jit(solution)/shard_map/ppermute | solution.py:547
  133.4 32.7 %collective-permute-start.10 = (bf16[1,2,1040,128]{3,2,1,0:T(8,128)(2,1)S(1)}, bf16[1,2,1040,128]{3,2,1,0:T(8,128)(2,1)S(1)}, u32[]{:S(2)}, u32[]{:S(2)}) collective-permute-start(bf16[1,2,1040,128]{3,2,1,0:T(8,128)(2,1)S(1)} %copy-done.10), channel_id=1, source_target_pairs={{0,2},{1,3},{2,0},{3,1},{4,6},{5,7},{6,4},{7,5},{8,10},{9,11},{10,... | collective-permute-start | bytes 1597448 | tf_op jit(solution)/shard_map/ppermute | solution.py:547
  133.5 43.6 %collective-permute-start.15 = (bf16[1,2,1040,128]{3,2,1,0:T(8,128)(2,1)S(1)}, bf16[1,2,1040,128]{3,2,1,0:T(8,128)(2,1)S(1)}, u32[]{:S(2)}, u32[]{:S(2)}) collective-permute-start(bf16[1,2,1040,128]{3,2,1,0:T(8,128)(2,1)S(1)} %copy-done.8), channel_id=1, source_target_pairs={{0,2},{1,3},{2,0},{3,1},{4,6},{5,7},{6,4},{7,5},{8,10},{9,11},{10,... | collective-permute-start | bytes 1597448 | tf_op jit(solution)/shard_map/ppermute | solution.py:547
  138.0 39.8 %collective-permute-start.24 = (f32[4,2,40,128]{3,2,1,0:T(8,128)S(1)}, f32[4,2,40,128]{3,2,1,0:T(8,128)S(1)}, u32[]{:S(2)}, u32[]{:S(2)}) collective-permute-start(f32[4,2,40,128]{3,2,1,0:T(8,128)S(1)} %get-tuple-element.24), channel_id=1, source_target_pairs={{0,0},{4,1},{8,2},{12,3},{1,4},{5,5},{9,6},{13,7},{2,8},{6,9},{10,... | collective-permute-start | bytes 491528 | tf_op jit(solution)/shard_map/ppermute | solution.py:551
  138.7 43.6 %collective-permute-start.25 = (f32[4,2,40,128]{3,2,1,0:T(8,128)S(1)}, f32[4,2,40,128]{3,2,1,0:T(8,128)S(1)}, u32[]{:S(2)}, u32[]{:S(2)}) collective-permute-start(f32[4,2,40,128]{3,2,1,0:T(8,128)S(1)} %get-tuple-element.25), channel_id=1, source_target_pairs={{4,0},{0,1},{12,2},{8,3},{5,4},{1,5},{13,6},{9,7},{6,8},{2,9},{14,... | collective-permute-start | bytes 491528 | tf_op jit(solution)/shard_map/ppermute | solution.py:551
  147.7 38.7 %collective-permute-start.26 = (f32[4,2,40,128]{3,2,1,0:T(8,128)S(1)}, f32[4,2,40,128]{3,2,1,0:T(8,128)S(1)}, u32[]{:S(2)}, u32[]{:S(2)}) collective-permute-start(f32[4,2,40,128]{3,2,1,0:T(8,128)S(1)} %get-tuple-element.26), channel_id=1, source_target_pairs={{8,0},{12,1},{0,2},{4,3},{9,4},{13,5},{1,6},{5,7},{10,8},{14,9},{2... | collective-permute-start | bytes 491528 | tf_op jit(solution)/shard_map/ppermute | solution.py:551
  166.1 20.9 %collective-permute-start.27 = (f32[4,2,40,128]{3,2,1,0:T(8,128)S(1)}, f32[4,2,40,128]{3,2,1,0:T(8,128)S(1)}, u32[]{:S(2)}, u32[]{:S(2)}) collective-permute-start(f32[4,2,40,128]{3,2,1,0:T(8,128)S(1)} %get-tuple-element.27), channel_id=1, source_target_pairs={{12,0},{8,1},{4,2},{0,3},{13,4},{9,5},{5,6},{1,7},{14,8},{10,9},{6... | collective-permute-start | bytes 491528 | tf_op jit(solution)/shard_map/ppermute | solution.py:551
  177.1 12.6 %collective-permute-start.6 = (bf16[1,1040,128]{2,1,0:T(8,128)(2,1)S(1)}, bf16[1,1040,128]{2,1,0:T(8,128)(2,1)S(1)}, u32[]{:S(2)}, u32[]{:S(2)}) collective-permute-start(bf16[1,1040,128]{2,1,0:T(8,128)(2,1)S(1)} %get-tuple-element.47), channel_id=1, source_target_pairs={{0,0},{1,4},{2,2},{3,6},{4,1},{5,5},{6,3},{7,7},{8,8},{9,12},{10,1... | collective-permute-start | bytes 798728 | tf_op jit(solution)/shard_map/ppermute | solution.py:575
  177.9 13.2 %collective-permute-start.7 = (bf16[1,1040,128]{2,1,0:T(8,128)(2,1)S(1)}, bf16[1,1040,128]{2,1,0:T(8,128)(2,1)S(1)}, u32[]{:S(2)}, u32[]{:S(2)}) collective-permute-start(bf16[1,1040,128]{2,1,0:T(8,128)(2,1)S(1)} %get-tuple-element.46), channel_id=1, source_target_pairs={{0,1},{1,5},{2,3},{3,7},{4,0},{5,4},{6,2},{7,6},{8,9},{9,13},{10,1... | collective-permute-start | bytes 798728 | tf_op jit(solution)/shard_map/ppermute | solution.py:575
  182.3 21.6 %collective-permute-start.8 = (bf16[1,1040,128]{2,1,0:T(8,128)(2,1)S(1)}, bf16[1,1040,128]{2,1,0:T(8,128)(2,1)S(1)}, u32[]{:S(2)}, u32[]{:S(2)}) collective-permute-start(bf16[1,1040,128]{2,1,0:T(8,128)(2,1)S(1)} %get-tuple-element.45), channel_id=1, source_target_pairs={{0,8},{1,12},{2,10},{3,14},{4,9},{5,13},{6,11},{7,15},{8,0},{9,4},... | collective-permute-start | bytes 798728 | tf_op jit(solution)/shard_map/ppermute | solution.py:575
  186.4 18.3 %collective-permute-start.11 = (bf16[1,1040,128]{2,1,0:T(8,128)(2,1)S(1)}, bf16[1,1040,128]{2,1,0:T(8,128)(2,1)S(1)}, u32[]{:S(2)}, u32[]{:S(2)}) collective-permute-start(bf16[1,1040,128]{2,1,0:T(8,128)(2,1)S(1)} %get-tuple-element.43), channel_id=1, source_target_pairs={{0,0},{1,4},{2,2},{3,6},{4,1},{5,5},{6,3},{7,7},{8,8},{9,12},{10,1... | collective-permute-start | bytes 798728 | tf_op jit(solution)/shard_map/ppermute | solution.py:575
  187.1 19.3 %collective-permute-start.12 = (bf16[1,1040,128]{2,1,0:T(8,128)(2,1)S(1)}, bf16[1,1040,128]{2,1,0:T(8,128)(2,1)S(1)}, u32[]{:S(2)}, u32[]{:S(2)}) collective-permute-start(bf16[1,1040,128]{2,1,0:T(8,128)(2,1)S(1)} %get-tuple-element.42), channel_id=1, source_target_pairs={{0,1},{1,5},{2,3},{3,7},{4,0},{5,4},{6,2},{7,6},{8,9},{9,13},{10,1... | collective-permute-start | bytes 798728 | tf_op jit(solution)/shard_map/ppermute | solution.py:575
  189.6 93.6 %copy-start.15 = (bf16[1,1040,128]{2,1,0:T(8,128)(2,1)}, bf16[1,1040,128]{2,1,0:T(8,128)(2,1)S(1)}, u32[]{:S(2)}) copy-start(bf16[1,1040,128]{2,1,0:T(8,128)(2,1)S(1)} %collective-permute-done.6.refs_0_) | copy-start | bytes 798724
  189.6 29.3 %collective-permute-start.13 = (bf16[1,1040,128]{2,1,0:T(8,128)(2,1)S(1)}, bf16[1,1040,128]{2,1,0:T(8,128)(2,1)S(1)}, u32[]{:S(2)}, u32[]{:S(2)}) collective-permute-start(bf16[1,1040,128]{2,1,0:T(8,128)(2,1)S(1)} %get-tuple-element.41), channel_id=1, source_target_pairs={{0,8},{1,12},{2,10},{3,14},{4,9},{5,13},{6,11},{7,15},{8,0},{9,4},... | collective-permute-start | bytes 798728 | tf_op jit(solution)/shard_map/ppermute | solution.py:575
  191.1 92.1 %copy-start.17 = (bf16[1,1040,128]{2,1,0:T(8,128)(2,1)}, bf16[1,1040,128]{2,1,0:T(8,128)(2,1)S(1)}, u32[]{:S(2)}) copy-start(bf16[1,1040,128]{2,1,0:T(8,128)(2,1)S(1)} %collective-permute-done.7.refs_1_) | copy-start | bytes 798724
  191.1 41.6 %collective-permute-start.14 = (bf16[1,1040,128]{2,1,0:T(8,128)(2,1)S(1)}, bf16[1,1040,128]{2,1,0:T(8,128)(2,1)S(1)}, u32[]{:S(2)}, u32[]{:S(2)}) collective-permute-start(bf16[1,1040,128]{2,1,0:T(8,128)(2,1)S(1)} %get-tuple-element.40), channel_id=1, source_target_pairs={{0,9},{1,13},{2,11},{3,15},{4,8},{5,12},{6,10},{7,14},{8,1},{9,5},... | collective-permute-start | bytes 798728 | tf_op jit(solution)/shard_map/ppermute | solution.py:575
  204.0 79.3 %copy-start.19 = (bf16[1,1040,128]{2,1,0:T(8,128)(2,1)}, bf16[1,1040,128]{2,1,0:T(8,128)(2,1)S(1)}, u32[]{:S(2)}) copy-start(bf16[1,1040,128]{2,1,0:T(8,128)(2,1)S(1)} %collective-permute-done.8.refs_2_) | copy-start | bytes 798724
  204.0 32.3 %collective-permute-start.16 = (bf16[1,1040,128]{2,1,0:T(8,128)(2,1)S(1)}, bf16[1,1040,128]{2,1,0:T(8,128)(2,1)S(1)}, u32[]{:S(2)}, u32[]{:S(2)}) collective-permute-start(bf16[1,1040,128]{2,1,0:T(8,128)(2,1)S(1)} %get-tuple-element.39), channel_id=1, source_target_pairs={{0,0},{1,4},{2,2},{3,6},{4,1},{5,5},{6,3},{7,7},{8,8},{9,12},{10,1... | collective-permute-start | bytes 798728 | tf_op jit(solution)/shard_map/ppermute | solution.py:575
  204.7 78.6 %copy-start.21 = (bf16[1,1040,128]{2,1,0:T(8,128)(2,1)}, bf16[1,1040,128]{2,1,0:T(8,128)(2,1)S(1)}, u32[]{:S(2)}) copy-start(bf16[1,1040,128]{2,1,0:T(8,128)(2,1)S(1)} %collective-permute-done.11.refs_0_) | copy-start | bytes 798724
  204.7 31.7 %collective-permute-start.17 = (bf16[1,1040,128]{2,1,0:T(8,128)(2,1)S(1)}, bf16[1,1040,128]{2,1,0:T(8,128)(2,1)S(1)}, u32[]{:S(2)}, u32[]{:S(2)}) collective-permute-start(bf16[1,1040,128]{2,1,0:T(8,128)(2,1)S(1)} %get-tuple-element.38), channel_id=1, source_target_pairs={{0,1},{1,5},{2,3},{3,7},{4,0},{5,4},{6,2},{7,6},{8,9},{9,13},{10,1... | collective-permute-start | bytes 798728 | tf_op jit(solution)/shard_map/ppermute | solution.py:575
  206.4 31.9 %collective-permute-start.18 = (bf16[1,1040,128]{2,1,0:T(8,128)(2,1)S(1)}, bf16[1,1040,128]{2,1,0:T(8,128)(2,1)S(1)}, u32[]{:S(2)}, u32[]{:S(2)}) collective-permute-start(bf16[1,1040,128]{2,1,0:T(8,128)(2,1)S(1)} %get-tuple-element.37), channel_id=1, source_target_pairs={{0,8},{1,12},{2,10},{3,14},{4,9},{5,13},{6,11},{7,15},{8,0},{9,4},... | collective-permute-start | bytes 798728 | tf_op jit(solution)/shard_map/ppermute | solution.py:575
  218.9 42.2 %collective-permute-start.19 = (bf16[1,1040,128]{2,1,0:T(8,128)(2,1)S(1)}, bf16[1,1040,128]{2,1,0:T(8,128)(2,1)S(1)}, u32[]{:S(2)}, u32[]{:S(2)}) collective-permute-start(bf16[1,1040,128]{2,1,0:T(8,128)(2,1)S(1)} %get-tuple-element.36), channel_id=1, source_target_pairs={{0,9},{1,13},{2,11},{3,15},{4,8},{5,12},{6,10},{7,14},{8,1},{9,5},... | collective-permute-start | bytes 798728 | tf_op jit(solution)/shard_map/ppermute | solution.py:575
  232.6 73.4 %collective-permute-start.1 = (bf16[1,1040,128]{2,1,0:T(8,128)(2,1)}, bf16[1,1040,128]{2,1,0:T(8,128)(2,1)}, u32[]{:S(2)}, u32[]{:S(2)}) collective-permute-start(bf16[1,1040,128]{2,1,0:T(8,128)(2,1)} %get-tuple-element.51), channel_id=1, source_target_pairs={{0,0},{1,4},{2,2},{3,6},{4,1},{5,5},{6,3},{7,7},{8,8},{9,12},{10,1... | collective-permute-start | bytes 798728 | tf_op jit(solution)/shard_map/ppermute | solution.py:575
  236.3 69.8 %collective-permute-start.2 = (bf16[1,1040,128]{2,1,0:T(8,128)(2,1)}, bf16[1,1040,128]{2,1,0:T(8,128)(2,1)}, u32[]{:S(2)}, u32[]{:S(2)}) collective-permute-start(bf16[1,1040,128]{2,1,0:T(8,128)(2,1)} %get-tuple-element.50), channel_id=1, source_target_pairs={{0,1},{1,5},{2,3},{3,7},{4,0},{5,4},{6,2},{7,6},{8,9},{9,13},{10,1... | collective-permute-start | bytes 798728 | tf_op jit(solution)/shard_map/ppermute | solution.py:575
  236.3 69.7 %collective-permute-start.3 = (bf16[1,1040,128]{2,1,0:T(8,128)(2,1)}, bf16[1,1040,128]{2,1,0:T(8,128)(2,1)}, u32[]{:S(2)}, u32[]{:S(2)}) collective-permute-start(bf16[1,1040,128]{2,1,0:T(8,128)(2,1)} %get-tuple-element.49), channel_id=1, source_target_pairs={{0,8},{1,12},{2,10},{3,14},{4,9},{5,13},{6,11},{7,15},{8,0},{9,4},... | collective-permute-start | bytes 798728 | tf_op jit(solution)/shard_map/ppermute | solution.py:575
  238.4 67.7 %collective-permute-start.4 = (bf16[1,1040,128]{2,1,0:T(8,128)(2,1)}, bf16[1,1040,128]{2,1,0:T(8,128)(2,1)}, u32[]{:S(2)}, u32[]{:S(2)}) collective-permute-start(bf16[1,1040,128]{2,1,0:T(8,128)(2,1)} %get-tuple-element.48), channel_id=1, source_target_pairs={{0,9},{1,13},{2,11},{3,15},{4,8},{5,12},{6,10},{7,14},{8,1},{9,5},... | collective-permute-start | bytes 798728 | tf_op jit(solution)/shard_map/ppermute | solution.py:575
  261.2 39.8 %collective-permute-start.9 = (bf16[1,1040,128]{2,1,0:T(8,128)(2,1)}, bf16[1,1040,128]{2,1,0:T(8,128)(2,1)}, u32[]{:S(2)}, u32[]{:S(2)}) collective-permute-start(bf16[1,1040,128]{2,1,0:T(8,128)(2,1)} %get-tuple-element.44), channel_id=1, source_target_pairs={{0,9},{1,13},{2,11},{3,15},{4,8},{5,12},{6,10},{7,14},{8,1},{9,5},... | collective-permute-start | bytes 798728 | tf_op jit(solution)/shard_map/ppermute | solution.py:575
  (42 other events, 848.4 us)
